TPU v7x, 512 devices: a whole 4x4x16 slice. The times are simulated.
512 devices in a mesh: mem: 8 (over z_lo), lon: 64 (over z_hi, y, x, core).
Axes of the slice: x: 4, y: 4, z: 16 (z_hi: 2, z_lo: 8; z = z_hi * 8 + z_lo), core: 2. Of those that a mesh axis runs over, the one named last changes fastest.
Arguments:
- latent: bfloat16 [48, 8, 2880, 78], P('mem', None, 'lon'), may hold values from -6 to 6
- conv_weight: bfloat16 [3, 3, 78, 78], replicated, may hold values from -0.21875 to 0.21875
- conv_bias: float32 [78], replicated, may hold values from -3 to 3
- obs_cell: int32 [131072], P('lon'), may hold values from 0 to 28079
- obs_value: float32 [131072], P('lon'), may hold values from -8 to 8
- obs_weight: float32 [131072], P('lon'), may hold values from 0.25 to 4
- obs_list: int32 [8, 2880, 64], P('mem', 'lon'), may hold values from 0 to 6143
Outputs:
- analysis: float32 [48, 8, 2880, 78], P(None, 'mem', 'lon')
All inputs are finite; a program needn't handle non-finite values.
Results may differ from a plain program's by a relative error of at most 0.0046.
Values may be sent and summed in bfloat16 or wider, within the bound.
A program may use at most 64 MiB of HBM per device.

v0:
```python
import functools

import jax
import jax.numpy as jnp
from jax import lax
from jax.experimental import pallas as pl
from jax.experimental.pallas import tpu as pltpu
from jax.sharding import PartitionSpec as P

SWEEPS = 6
MEM = 8
MEMBERS = 48
CHANS = 78
WIDTH = 45
LAT = 8
OWN = 6
PACK = 3
SETS = OWN // PACK
OBS = 2048
OBS_COL = 64
LANES = 128
GROUP = 5
GROUPS = WIDTH // GROUP
CELLS = WIDTH * LAT
BAND = 384
WIDE = 2 * LANES
SLOT = 48
F32 = jnp.float32
BF16 = jnp.bfloat16
MESH = pl.DeviceIdType.MESH


def dot(left, right):
    return jnp.dot(left, right, preferred_element_type=F32)


def silu(v):
    return v / (1.0 + jnp.exp(-v))


def split(v):
    high = v.astype(BF16)
    return high, (v - high.astype(F32)).astype(BF16)


def combine(parts):
    rows = parts.shape[0]
    cube = parts.reshape(rows // LAT, LAT, 3 * WIDE)
    spot = lax.broadcasted_iota(jnp.int32, (rows // LAT, LAT, WIDE), 1)
    above = pltpu.roll(cube[:, :, :WIDE], 1, 1)
    below = pltpu.roll(cube[:, :, 2 * WIDE :], LAT - 1, 1)
    total = cube[:, :, WIDE : 2 * WIDE]
    total = total + jnp.where(spot > 0, above, 0.0) + jnp.where(spot < LAT - 1, below, 0.0)
    return total.reshape(rows, WIDE)


def exchange_kernel(
    lat_ref, w_ref, bias_ref, cell_ref, value_ref, weight_ref,
    blocks, stats, states,
    field, act, wpad, taps, total, halves, turned, cellp, cellc, own, edge_out, edge_in, rows_out,
    edge_sent, edge_got, stat_sent, stat_got, line_sent, sib_sent, outer_sent, block_got,
    state_sent, state_got,
):
    m = lax.axis_index("mem")
    t = lax.axis_index("lon")
    tiles = lax.axis_size("lon")
    core = lax.rem(t, 2)
    left = lax.rem(t + tiles - 1, tiles)
    right = lax.rem(t + 1, tiles)
    outer = jnp.where(core == 0, left, right)
    inner = jnp.where(core == 0, right, left)

    barrier = pltpu.get_barrier_semaphore()
    for lon in (left, right):
        pl.semaphore_signal(barrier, inc=1, device_id={"lon": lon}, device_id_type=MESH)
    for step in range(1, MEM):
        pl.semaphore_signal(
            barrier, inc=1, device_id={"mem": lax.rem(m + step, MEM)}, device_id_type=MESH
        )

    edge_out[...] = jnp.zeros_like(edge_out)
    for side, column in ((0, WIDTH - 1), (1, 0)):
        edge = lat_ref[:, column].astype(F32).reshape(OWN * LAT, CHANS)
        edge_out[side, :, :CHANS] = edge.astype(BF16)
    stats[1, 0] = value_ref[...]
    stats[1, 1] = weight_ref[...]
    pl.semaphore_wait(barrier, MEM + 1)

    edges = [
        pltpu.make_async_remote_copy(
            src_ref=edge_out.at[side],
            dst_ref=edge_in.at[side],
            send_sem=edge_sent.at[side],
            recv_sem=edge_got.at[side],
            device_id={"lon": lon},
            device_id_type=MESH,
        )
        for side, lon in ((0, right), (1, left))
    ]
    stat_copies = [
        pltpu.make_async_remote_copy(
            src_ref=stats.at[1],
            dst_ref=stats.at[2 * side],
            send_sem=stat_sent.at[side],
            recv_sem=stat_got.at[side],
            device_id={"lon": lon},
            device_id_type=MESH,
        )
        for side, lon in ((0, right), (1, left))
    ]
    for copy in edges + stat_copies:
        copy.start()

    wpad[...] = jnp.zeros_like(wpad)
    lane = lax.broadcasted_iota(jnp.int32, (LANES, WIDE), 1)
    depth = lax.broadcasted_iota(jnp.int32, (LANES, WIDE), 0)
    blank = jnp.zeros((LANES, LANES), F32)
    for a in range(3):
        for b in range(3):
            wpad[:CHANS, :CHANS] = w_ref[a, b].astype(F32)
            whole = jnp.concatenate([wpad[...], blank], axis=1)
            for r in range(PACK):
                moved = whole if r == 0 else pltpu.roll(whole, CHANS * r, 1)
                taps[r, b * LANES : (b + 1) * LANES, a * WIDE : (a + 1) * WIDE] = moved.astype(BF16)
    for r in range(PACK):
        same = jnp.where((lane - CHANS * r == depth) & (depth < CHANS), 1.0, 0.0)
        taps[r, 3 * LANES :, :WIDE] = jnp.zeros((LANES, WIDE), BF16)
        taps[r, 3 * LANES :, WIDE : 2 * WIDE] = same.astype(BF16)
        taps[r, 3 * LANES :, 2 * WIDE :] = jnp.zeros((LANES, WIDE), BF16)
    wpad[:1, :CHANS] = bias_ref[...]
    bias = jnp.concatenate([wpad[:8, :], blank[:8, :]], axis=1)
    bias = bias + pltpu.roll(bias, CHANS, 1) + pltpu.roll(bias, 2 * CHANS, 1)
    bias = jnp.where(lane[:8, :] < PACK * CHANS, bias, 0.0)[:1, :]

    flat = cell_ref[...]
    pixel = jnp.floor((flat.astype(F32) + 0.5) * (1.0 / CHANS)).astype(jnp.int32)
    row = jnp.floor((pixel.astype(F32) + 0.5) * (1.0 / WIDTH)).astype(jnp.int32)
    cellc[...] = flat - CHANS * pixel
    cellp[...] = (pixel - WIDTH * row) * LAT + row

    field[...] = jnp.zeros_like(field)
    for k in range(OWN):
        field[k, LAT : LAT + CELLS, :CHANS] = lat_ref[k].astype(F32).reshape(CELLS, CHANS)
    act[...] = silu(field[...])

    span = CELLS + LAT
    for g in range(SETS):
        parts = None
        for r in range(PACK):
            k = PACK * g + r
            sides = [act[k, LAT * b : LAT * b + span, :].astype(BF16) for b in range(3)]
            sides.append(field[k, LAT : LAT + span, :].astype(BF16))
            part = dot(jnp.concatenate(sides, axis=1), taps[r])
            parts = part if parts is None else parts + part
        total[g, :span] = combine(parts) + bias
        total[g, span:] = jnp.zeros((BAND - span, WIDE), F32)

    for side, copy in enumerate(edges):
        copy.wait_recv()
        turn = silu(edge_in[side].astype(F32)).astype(BF16).astype(F32)
        parts = None
        for r in range(PACK):
            pick = [turn[(PACK * g + r) * LAT : (PACK * g + r + 1) * LAT] for g in range(SETS)]
            tap = 2 * side
            part = dot(
                jnp.concatenate(pick, axis=0).astype(BF16), taps[r, tap * LANES : (tap + 1) * LANES]
            )
            parts = part if parts is None else parts + part
        extra = combine(parts)
        first = 0 if side == 0 else CELLS - LAT
        for g in range(SETS):
            total[g, first : first + LAT] += extra[g * LAT : (g + 1) * LAT]

    total[...] = total[...].astype(BF16).astype(F32)
    for g in range(SETS):
        halves[2 * g] = total[g, :, :LANES]
        halves[2 * g + 1] = total[g, :, LANES:]
        turned[g * WIDE : (g + 1) * WIDE] = total[g].T.astype(BF16)

    place = lax.broadcasted_iota(jnp.int32, (BAND, LANES), 0)
    channel = lax.broadcasted_iota(jnp.int32, (WIDE, WIDE), 0)

    def choose(pair, carry):
        first = cellp[pl.ds(2 * pair, 1), :]
        second = cellp[pl.ds(2 * pair + 1, 1), :]
        hot = jnp.concatenate(
            [
                jnp.where(place == first, 1.0, 0.0).astype(BF16),
                jnp.where(place == second, 1.0, 0.0).astype(BF16),
            ],
            axis=1,
        )
        chans = jnp.concatenate(
            [cellc[pl.ds(2 * pair, 1), :], cellc[pl.ds(2 * pair + 1, 1), :]], axis=1
        )
        for g in range(SETS):
            cells = dot(turned[g * WIDE : (g + 1) * WIDE, :], hot)
            for r in range(PACK):
                low, high = CHANS * r // 8 * 8, -(-CHANS * (r + 1) // 8) * 8
                mask = channel[low:high] - CHANS * r == chans
                found = jnp.sum(jnp.where(mask, cells[low:high], 0.0), axis=0, keepdims=True)
                spot = (PACK * g + r) * 16 + 2 * pair
                own[pl.ds(spot, 1), :] = found[:, :LANES]
                own[pl.ds(spot + 1, 1), :] = found[:, LANES:]
        return carry

    lax.fori_loop(0, OBS // WIDE, choose, 0)
    blocks[1, m] = own[...].astype(BF16)

    def hop(slot, kind, way, block, to):
        return pltpu.make_async_remote_copy(
            src_ref=blocks.at[slot, block],
            dst_ref=blocks.at[slot, block],
            send_sem=line_sent.at[kind, way, block],
            recv_sem=block_got.at[slot, block],
            device_id={"mem": to},
            device_id_type=MESH,
        )

    def across(block):
        return pltpu.make_async_remote_copy(
            src_ref=blocks.at[1, block],
            dst_ref=blocks.at[2 * core, block],
            send_sem=sib_sent.at[block],
            recv_sem=block_got.at[2 * core, block],
            device_id={"lon": inner},
            device_id_type=MESH,
        )

    def arrival(slot, block):
        return pltpu.make_async_remote_copy(
            src_ref=blocks.at[1, block],
            dst_ref=blocks.at[slot, block],
            send_sem=outer_sent.at[0],
            recv_sem=block_got.at[slot, block],
            device_id={"lon": inner},
            device_id_type=MESH,
        )

    far = pltpu.make_async_remote_copy(
        src_ref=blocks.at[1, m],
        dst_ref=blocks.at[2 - 2 * core, m],
        send_sem=outer_sent.at[0],
        recv_sem=block_got.at[2 - 2 * core, m],
        device_id={"lon": outer},
        device_id_type=MESH,
    )
    far.start()

    up, down = jnp.minimum(m + 1, MEM - 1), jnp.maximum(m - 1, 0)

    def relay(kind, step):
        slot = 1 if kind == 0 else 2 * core
        low, high = m - step, m + step

        @pl.when(low >= 0)
        def _():
            block = jnp.maximum(low, 0)
            if step > 0 or kind == 1:
                arrival(slot, block).wait_recv()

            @pl.when(m < MEM - 1)
            def _():
                hop(slot, kind, 0, block, up).start()

            if kind == 0:
                across(block).start()

        @pl.when(high < MEM)
        def _():
            block = jnp.minimum(high, MEM - 1)
            if step > 0:
                arrival(slot, block).wait_recv()

            @pl.when(m > 0)
            def _():
                hop(slot, kind, 1, block, down).start()

            if kind == 0 and step > 0:
                across(block).start()

    relay(0, 0)
    for i in range(LAT):
        for g in range(SETS):
            for h in range(2):
                half = 2 * g + h
                rows_out[i, :, half * LANES : (half + 1) * LANES] = halves[
                    half, pl.ds(i, SLOT, stride=LAT), :
                ].astype(BF16)
    states[m] = rows_out[m]
    for step in range(1, MEM + 1):
        if step < MEM:
            relay(0, step)
        relay(1, step - 1)

    def row_copy(to, source):
        return pltpu.make_async_remote_copy(
            src_ref=rows_out.at[to],
            dst_ref=states.at[source],
            send_sem=state_sent.at[to],
            recv_sem=state_got.at[source],
            device_id={"mem": to},
            device_id_type=MESH,
        )

    for step in range(1, MEM):
        row_copy(lax.rem(m + step, MEM), m).start()

    for block in range(MEM):
        arrival(2 - 2 * core, block).wait_recv()
    for copy in stat_copies:
        copy.wait()
    for copy in edges:
        copy.wait_send()
    far.wait_send()
    for block in range(MEM):
        across(block).wait_send()
    for kind in range(2):
        slot = 1 if kind == 0 else 2 * core
        for block in range(MEM):

            @pl.when((m < MEM - 1) & (block <= m))
            def _():
                hop(slot, kind, 0, block, up).wait_send()

            @pl.when((m > 0) & (block >= m))
            def _():
                hop(slot, kind, 1, block, down).wait_send()

    for step in range(1, MEM):
        other = lax.rem(m + step, MEM)
        row_copy(other, other).wait_recv()
        row_copy(other, other).wait_send()


def exchange(lat, weights, bias, cell, value, weight):
    vmem = pl.BlockSpec(memory_space=pltpu.VMEM)
    dma = pltpu.SemaphoreType.DMA
    return pl.pallas_call(
        exchange_kernel,
        out_shape=[
            jax.ShapeDtypeStruct((3, MEM, OWN * 16, LANES), BF16),
            jax.ShapeDtypeStruct((3, 2, 16, LANES), F32),
            jax.ShapeDtypeStruct((MEM, SLOT, SETS * WIDE), BF16),
        ],
        in_specs=[vmem] * 6,
        out_specs=[vmem] * 3,
        scratch_shapes=[
            pltpu.VMEM((OWN, BAND, LANES), F32),
            pltpu.VMEM((OWN, BAND, LANES), F32),
            pltpu.VMEM((LANES, LANES), F32),
            pltpu.VMEM((PACK, 4 * LANES, 3 * WIDE), BF16),
            pltpu.VMEM((SETS, BAND, WIDE), F32),
            pltpu.VMEM((2 * SETS, BAND, LANES), F32),
            pltpu.VMEM((SETS * WIDE, BAND), BF16),
            pltpu.VMEM((16, LANES), jnp.int32),
            pltpu.VMEM((16, LANES), jnp.int32),
            pltpu.VMEM((OWN * 16, LANES), F32),
            pltpu.VMEM((2, OWN * LAT, LANES), BF16),
            pltpu.VMEM((2, OWN * LAT, LANES), BF16),
            pltpu.VMEM((LAT, SLOT, SETS * WIDE), BF16),
            dma((2,)),
            dma((2,)),
            dma((2,)),
            dma((2,)),
            dma((2, 2, MEM)),
            dma((MEM,)),
            dma((1,)),
            dma((3, MEM)),
            dma((MEM,)),
            dma((MEM,)),
        ],
        compiler_params=pltpu.CompilerParams(
            collective_id=0, has_side_effects=True, vmem_limit_bytes=48 * 2**20
        ),
    )(lat, weights, bias, cell, value, weight)


BATCH = 3


def spread(piece):
    return jnp.concatenate([piece] * GROUP + [jnp.zeros((16, WIDE), BF16)], axis=0)


def analysis_kernel(
    list_ref, blocks, stats, states, out, flat, table, picked, columns, diagonal, unpack, done
):
    lane = lax.broadcasted_iota(jnp.int32, (1, WIDE), 1)

    row = lax.broadcasted_iota(jnp.int32, (WIDE, WIDE), 0)
    col = lax.broadcasted_iota(jnp.int32, (WIDE, WIDE), 1)
    mask = jnp.zeros((WIDE, WIDE), F32)
    for s in range(GROUP):
        low, high = s * MEMBERS, (s + 1) * MEMBERS
        mask = jnp.where((row >= low) & (row < high) & (col >= low) & (col < high), 1.0, mask)
    diagonal[...] = mask.astype(BF16)
    row = lax.broadcasted_iota(jnp.int32, (WIDE, LANES), 0)
    col = lax.broadcasted_iota(jnp.int32, (WIDE, LANES), 1)
    for r in range(PACK):
        unpack[:, r * LANES : (r + 1) * LANES] = jnp.where(
            (row - CHANS * r == col) & (col < CHANS), 1.0, 0.0
        ).astype(BF16)

    for s in range(3):
        flat[s * MEM * OWN * 16 : (s + 1) * MEM * OWN * 16] = (
            blocks[s].astype(F32).reshape(MEM * OWN * 16, LANES)
        )
    blank = jnp.zeros((LANES - MEMBERS - 2, LANES), F32)

    def turn(k, carry):
        for s in range(3):
            cells = flat[pl.ds(s * MEM * OWN * 16 + k, MEMBERS, stride=16), :]
            extra = [stats[s, kind, pl.ds(k, 1), :] for kind in range(2)]
            whole = jnp.concatenate([cells] + extra + [blank], axis=0)
            start = pl.multiple_of(s * OBS + k * LANES, LANES)
            table[pl.ds(start, LANES), :] = whole.T
        return carry

    lax.fori_loop(0, 16, turn, 0)

    for source in range(MEM):
        for g in range(SETS):
            parts = dot(states[source, :, g * WIDE : (g + 1) * WIDE], unpack[...])
            for r in range(PACK):
                columns[pl.ds(source * OWN + g * PACK + r, SLOT, stride=MEMBERS), :] = parts[
                    :, r * LANES : (r + 1) * LANES
                ]

    eye = jnp.zeros((MEMBERS, WIDE), F32)
    row48 = lax.broadcasted_iota(jnp.int32, (MEMBERS, WIDE), 0)
    col48 = lax.broadcasted_iota(jnp.int32, (MEMBERS, WIDE), 1)
    for s in range(GROUP):
        eye = jnp.where(col48 - MEMBERS * s == row48, 1.0, eye)

    def block_sum(pieces):
        return dot(jnp.concatenate(pieces, axis=0), diagonal[...])

    def gather(column, carry):
        base = column * OBS_COL
        for o in range(OBS_COL):
            index = list_ref[column, o]
            picked[pl.ds(base + o, 1), :] = table[pl.ds(index, 1), :]
        return carry

    lax.fori_loop(0, WIDTH, gather, 0)

    near = lax.broadcasted_iota(jnp.int32, (OBS_COL, LANES), 1)
    block48 = [(lane >= s * MEMBERS) & (lane < (s + 1) * MEMBERS) for s in range(GROUP)]

    def start(q):
        placed = proj = rate = None
        for s in range(GROUP):
            first = pl.multiple_of((q * GROUP + s) * OBS_COL, OBS_COL)
            rows = picked[pl.ds(first, OBS_COL), :]
            ens = jnp.where(near < MEMBERS, rows, 0.0)
            mean = jnp.sum(ens, axis=1, keepdims=True) * (1.0 / MEMBERS)
            pert = jnp.where(near < MEMBERS, ens - mean, 0.0)
            weight = rows[:, MEMBERS + 1 : MEMBERS + 2]
            scaled = weight * (rows[:, MEMBERS : MEMBERS + 1] - mean)
            wide = jnp.concatenate([pert, jnp.zeros((OBS_COL, LANES), F32)], axis=1)
            if s > 0:
                wide = pltpu.roll(wide, s * MEMBERS, 1)
            part = jnp.sum(wide * scaled, axis=0, keepdims=True)
            spread_weight = jnp.where(block48[s], weight, 0.0)
            placed = wide if placed is None else placed + wide
            proj = part if proj is None else proj + part
            rate = spread_weight if rate is None else rate + spread_weight
        high, low = split(placed)
        scaled_high, scaled_low = split(placed * rate)
        square = lax.dot_general(
            jnp.concatenate([scaled_high, scaled_low, scaled_high], axis=0),
            jnp.concatenate([high, high, low], axis=0),
            (((0,), (0,)), ((), ())),
            preferred_element_type=F32,
        )
        gram = (MEMBERS - 1.0) * eye
        for s in range(GROUP):
            piece = square[s * MEMBERS : (s + 1) * MEMBERS]
            gram = gram + jnp.where(block48[s], piece, 0.0)
        trace = jnp.sum(gram * eye, axis=0, keepdims=True)
        one, rest = split(trace)
        two, three = split(trace - one.astype(F32))
        del rest
        sums = block_sum([one, two, three, jnp.zeros((13, WIDE), BF16)])
        scale = sums[0:1] + sums[1:2] + sums[2:3]
        scale = jnp.where(lane < GROUP * MEMBERS, scale, 1.0)
        return gram / scale, scale, proj

    def times(parts, high, low):
        count = len(parts)
        first = dot(jnp.concatenate([x for pair in parts for x in pair], axis=0), high)
        second = dot(jnp.concatenate([pair[0] for pair in parts], axis=0), low)
        size = parts[0][0].shape[0]
        return [
            first[2 * n * size : (2 * n + 1) * size]
            + first[(2 * n + 1) * size : (2 * n + 2) * size]
            + second[n * size : (n + 1) * size]
            for n in range(count)
        ]

    def lay(pair):
        return [spread(piece) * diagonal[...] for piece in pair]

    def batch(index, carry):
        qs = [index * BATCH + n for n in range(BATCH)]
        state = [start(q) for q in qs]
        ratio = [item[0] for item in state]
        inverse = [None] * BATCH
        for sweep in range(SWEEPS):
            factor = [1.5 * eye - 0.5 * r for r in ratio]
            pairs = [split(f) for f in factor]
            weights = [lay(pair) for pair in pairs]
            for n in range(BATCH):
                todo = []
                if sweep < SWEEPS - 1:
                    todo.append(split(ratio[n]))
                if sweep > 0:
                    todo.append(split(inverse[n]))
                products = times(todo, *weights[n])
                inverse[n] = products[-1] if sweep > 0 else factor[n]
                ratio[n] = products[0]
            if sweep < SWEEPS - 1:
                ratio = [times([split(ratio[n])], *weights[n])[0] for n in range(BATCH)]
        for n in range(BATCH):
            q = qs[n]
            _, scale, proj = state[n]
            root = inverse[n] * lax.rsqrt(scale)
            weights = lay(split(root))
            vector = proj
            for _ in range(2):
                high, low = split(jnp.broadcast_to(vector, (16, WIDE)))
                vector = times([(high, low)], *weights)[0][:1]
            transform = (MEMBERS - 1.0) ** 0.5 * root + vector
            high, low = split(transform)
            sums = block_sum([high, low])
            sums = sums[:MEMBERS] + sums[MEMBERS:]
            transform = transform + (1.0 - sums) * (1.0 / MEMBERS)
            high, low = split(transform)
            first = pl.multiple_of(q * GROUP * MEMBERS, 16)
            field = columns[pl.ds(first, WIDE), :].astype(BF16)
            both = [spread(piece) * diagonal[...] for piece in (high, low)]
            result = dot(both[0], field) + dot(both[1], field)
            for s in range(GROUP):
                piece = result[s * MEMBERS : (s + 1) * MEMBERS]
                done[pl.ds(q * GROUP + s, MEMBERS, stride=WIDTH), :] = piece
        return carry

    lax.fori_loop(0, GROUPS // BATCH, batch, 0)
    out[...] = done[:, :CHANS]


def analysis(lists, blocks, stats, states):
    vmem = pl.BlockSpec(memory_space=pltpu.VMEM)
    return pl.pallas_call(
        analysis_kernel,
        out_shape=jax.ShapeDtypeStruct((MEMBERS * WIDTH, CHANS), F32),
        in_specs=[pl.BlockSpec(memory_space=pltpu.SMEM), vmem, vmem, vmem],
        out_specs=vmem,
        scratch_shapes=[
            pltpu.VMEM((3 * MEM * OWN * 16, LANES), F32),
            pltpu.VMEM((3 * OBS, LANES), F32),
            pltpu.VMEM((WIDTH * OBS_COL, LANES), F32),
            pltpu.VMEM((SLOT * MEMBERS, LANES), F32),
            pltpu.VMEM((WIDE, WIDE), BF16),
            pltpu.VMEM((WIDE, PACK * LANES), BF16),
            pltpu.VMEM((MEMBERS * WIDTH, LANES), F32),
        ],
        compiler_params=pltpu.CompilerParams(vmem_limit_bytes=48 * 2**20),
    )(lists, blocks, stats, states)


def local(latent, conv_weight, conv_bias, obs_cell, obs_value, obs_weight, obs_list):
    blocks, stats, states = exchange(
        jnp.transpose(latent, (0, 2, 1, 3)),
        conv_weight,
        conv_bias.reshape(1, CHANS),
        obs_cell.reshape(16, LANES),
        obs_value.reshape(16, LANES),
        obs_weight.reshape(16, LANES),
    )
    result = analysis(obs_list.reshape(WIDTH, OBS_COL), blocks, stats, states)
    return jnp.transpose(result.reshape(MEMBERS, WIDTH, 1, CHANS), (0, 2, 1, 3))


def solution(mesh):
    placed = (
        P("mem", None, "lon", None),
        P(),
        P(),
        P("lon"),
        P("lon"),
        P("lon"),
        P("mem", "lon", None),
    )
    return jax.shard_map(
        local, mesh=mesh, in_specs=placed, out_specs=P(None, "mem", "lon", None), check_vma=False
    )
```

profile of v0, /device:TPU:224, one launch (start us, length us, event | category | flops | bytes accessed | tf_op | source)
XLA Modules:
  0.0 95.7 jit_solution(845294049615713502)
XLA Ops:
  0.0 0.7 copy.12
  0.7 0.0 copy-start
  0.7 1.0 %copy-done = bf16[6,8,45,78]{3,1,2,0:T(8,128)(2,1)S(1)} copy-done((bf16[6,8,45,78]{3,1,2,0:T(8,128)(2,1)S(1)}, bf16[6,8,45,78]{3,1,2,0:T(8,128)(2,1)}, u32[]{:S(2)}) %copy-start) | copy-done | bytes 336984
  1.8 0.0 copy-start.1
  1.8 0.9 copy-done.1
  2.7 0.0 copy-start.2
  2.7 0.7 copy-done.2
  3.4 0.0 copy-start.3
  3.4 0.7 copy-done.3
  4.1 0.0 copy-start.4
  4.1 0.7 copy-done.4
  4.8 0.0 copy-start.5
  4.8 0.7 copy-done.5
  5.5 68.5 %shard_map.73 = (bf16[3,8,96,128]{3,2,1,0:T(8,128)(2,1)S(1)}, f32[3,2,16,128]{3,2,1,0:T(8,128)S(1)}, bf16[8,48,512]{2,1,0:T(8,128)(2,1)S(1)}) custom-call(bf16[6,45,8,78]{3,2,1,0:T(8,128)(2,1)S(1)} %bitcast.9, bf16[3,3,78,78]{3,2,1,0:T(8,128)(2,1)S(1)} %copy-done.1, f32[1,78]{1,0:T(1,128)S(1)} %bitcast.14, s32[16,128]{1,0:T(8,128)S(1)} %bitcast.11, ...), custom_call_target="tpu_custom_call" | custom-call | tf_op jit(solution)/shard_map/pallas_call | solution.py:339
  74.0 21.7 %shard_map.74 = f32[2160,78]{1,0:T(8,128)} custom-call(s32[45,64]{1,0:T(8,128)S(1)} %bitcast.10, bf16[3,8,96,128]{3,2,1,0:T(8,128)(2,1)S(1)} %get-tuple-element.8.blocks, f32[3,2,16,128]{3,2,1,0:T(8,128)S(1)} %get-tuple-element.9.stats, bf16[8,48,512]{2,1,0:T(8,128)(2,1)S(1)} %get-tuple-element.10.states), custom_call_target="tpu_custom_call" | custom-call | tf_op jit(solution)/shard_map/pallas_call | solution.py:555
Async XLA Ops:
  0.7 1.1 %copy-start = (bf16[6,8,45,78]{3,1,2,0:T(8,128)(2,1)S(1)}, bf16[6,8,45,78]{3,1,2,0:T(8,128)(2,1)}, u32[]{:S(2)}) copy-start(bf16[6,8,45,78]{3,1,2,0:T(8,128)(2,1)} %param.7) | copy-start | bytes 1010884
  1.8 0.9 copy-start.1
  2.7 0.7 copy-start.2
  3.4 0.7 copy-start.3
  4.1 0.7 copy-start.4
  4.8 0.7 copy-start.5
where the time goes:
time: 96.1 us; the launch traced here: 95.7 us
  Pallas kernels  90.2 us (94%)
  local copies, waits for them, and re-layouts  5.45 us (6%)
    pallas_call x1, Pallas kernels, exchange(): pl.pallas_call(exchange_kernel, out_shape=[jax.ShapeDtypeStruct((3, MEM,...  68.5 us
    pallas_call x1, Pallas kernels, analysis(): pl.pallas_call(analysis_kernel, out_shape=jax.ShapeDtypeStruct((MEMBERS *...  21.7 us
    unnamed x13, local copies, waits for them, and re-layouts  5.45 us

commit v1 on v0

v1 whole, which is shorter than its diff:
```python
import functools

import jax
import jax.numpy as jnp
from jax import lax
from jax.experimental import pallas as pl
from jax.experimental.pallas import tpu as pltpu
from jax.sharding import PartitionSpec as P

SWEEPS = 6
MEM = 8
MEMBERS = 48
CHANS = 78
WIDTH = 45
LAT = 8
OWN = 6
PACK = 3
SETS = OWN // PACK
OBS = 2048
OBS_COL = 64
LANES = 128
GROUP = 5
GROUPS = WIDTH // GROUP
CELLS = WIDTH * LAT
BAND = 384
WIDE = 2 * LANES
SLOT = 48
F32 = jnp.float32
BF16 = jnp.bfloat16
MESH = pl.DeviceIdType.MESH


def dot(left, right):
    return jnp.dot(left, right, preferred_element_type=F32)


def silu(v):
    return v / (1.0 + jnp.exp(-v))


def split(v):
    high = v.astype(BF16)
    return high, (v - high.astype(F32)).astype(BF16)


def combine(parts):
    rows = parts.shape[0]
    cube = parts.reshape(rows // LAT, LAT, 3 * WIDE)
    spot = lax.broadcasted_iota(jnp.int32, (rows // LAT, LAT, WIDE), 1)
    above = pltpu.roll(cube[:, :, :WIDE], 1, 1)
    below = pltpu.roll(cube[:, :, 2 * WIDE :], LAT - 1, 1)
    total = cube[:, :, WIDE : 2 * WIDE]
    total = total + jnp.where(spot > 0, above, 0.0) + jnp.where(spot < LAT - 1, below, 0.0)
    return total.reshape(rows, WIDE)


def exchange_kernel(
    lat_hbm, w_hbm, bias_hbm, cell_hbm, value_hbm, weight_hbm,
    blocks, stats, states, edges,
    lat_ref, w_ref, bias_ref, cell_ref, field, act, wpad, taps, total, halves, turned, cellp, cellc,
    own, edge_out, edge_in, rows_out, ends, ends_out,
    loaded, edge_sent, edge_got, stat_sent, stat_got, mate_sent, sib_sent, outer_sent, block_got,
    state_sent, state_got, end_sent, end_got,
):
    m = lax.axis_index("mem")
    t = lax.axis_index("lon")
    tiles = lax.axis_size("lon")
    core = lax.rem(t, 2)
    left = lax.rem(t + tiles - 1, tiles)
    right = lax.rem(t + 1, tiles)
    outer = jnp.where(core == 0, left, right)
    inner = jnp.where(core == 0, right, left)
    mine, theirs = 2 * core, 2 - 2 * core
    far = lax.rem(jnp.where(core == 0, t, t + 1), tiles // 2) == 0

    barrier = pltpu.get_barrier_semaphore()
    for lon in (left, right):
        pl.semaphore_signal(barrier, inc=1, device_id={"lon": lon}, device_id_type=MESH)

    @pl.when(far)
    def _():
        for step in range(1, MEM):
            to = {"mem": lax.rem(m + step, MEM), "lon": outer}
            pl.semaphore_signal(barrier, inc=1, device_id=to, device_id_type=MESH)

    for step in range(1, MEM):
        to = {"mem": lax.rem(m + step, MEM)}
        pl.semaphore_signal(barrier, inc=1, device_id=to, device_id_type=MESH)

    loads = [
        pltpu.make_async_copy(source, target, loaded.at[n])
        for n, (source, target) in enumerate(
            (
                (lat_hbm, lat_ref),
                (w_hbm, w_ref),
                (bias_hbm, bias_ref),
                (cell_hbm, cell_ref),
                (value_hbm, stats.at[1, 0]),
                (weight_hbm, stats.at[1, 1]),
            )
        )
    ]
    for load in loads:
        load.start()

    edge_out[...] = jnp.zeros_like(edge_out)
    field[...] = jnp.zeros_like(field)
    wpad[...] = jnp.zeros_like(wpad)
    ends[...] = jnp.zeros_like(ends)
    for load in loads:
        load.wait()
    for side, column in ((0, WIDTH - 1), (1, 0)):
        edge = lat_ref[:, column].astype(F32).reshape(OWN * LAT, CHANS)
        edge_out[side, :, :CHANS] = edge.astype(BF16)

    lane = lax.broadcasted_iota(jnp.int32, (LANES, WIDE), 1)
    depth = lax.broadcasted_iota(jnp.int32, (LANES, WIDE), 0)
    blank = jnp.zeros((LANES, LANES), F32)
    for a in range(3):
        for b in range(3):
            wpad[:CHANS, :CHANS] = w_ref[a, b].astype(F32)
            whole = jnp.concatenate([wpad[...], blank], axis=1)
            for r in range(PACK):
                moved = whole if r == 0 else pltpu.roll(whole, CHANS * r, 1)
                taps[r, b * LANES : (b + 1) * LANES, a * WIDE : (a + 1) * WIDE] = moved.astype(BF16)
    for r in range(PACK):
        same = jnp.where((lane - CHANS * r == depth) & (depth < CHANS), 1.0, 0.0)
        taps[r, 3 * LANES :, :WIDE] = jnp.zeros((LANES, WIDE), BF16)
        taps[r, 3 * LANES :, WIDE : 2 * WIDE] = same.astype(BF16)
        taps[r, 3 * LANES :, 2 * WIDE :] = jnp.zeros((LANES, WIDE), BF16)
    wpad[:1, :CHANS] = bias_ref[...]
    bias = jnp.concatenate([wpad[:8, :], blank[:8, :]], axis=1)
    bias = bias + pltpu.roll(bias, CHANS, 1) + pltpu.roll(bias, 2 * CHANS, 1)
    bias = jnp.where(lane[:8, :] < PACK * CHANS, bias, 0.0)[:1, :]

    flat = cell_ref[...]
    pixel = jnp.floor((flat.astype(F32) + 0.5) * (1.0 / CHANS)).astype(jnp.int32)
    row = jnp.floor((pixel.astype(F32) + 0.5) * (1.0 / WIDTH)).astype(jnp.int32)
    cellc[...] = flat - CHANS * pixel
    cellp[...] = (pixel - WIDTH * row) * LAT + row

    pl.semaphore_wait(barrier, jnp.where(far, 2 * MEM, MEM + 1))

    edge_copies = [
        pltpu.make_async_remote_copy(
            src_ref=edge_out.at[side],
            dst_ref=edge_in.at[side],
            send_sem=edge_sent.at[side],
            recv_sem=edge_got.at[side],
            device_id={"lon": lon},
            device_id_type=MESH,
        )
        for side, lon in ((0, right), (1, left))
    ]
    stat_copies = [
        pltpu.make_async_remote_copy(
            src_ref=stats.at[1],
            dst_ref=stats.at[2 * side],
            send_sem=stat_sent.at[side],
            recv_sem=stat_got.at[side],
            device_id={"lon": lon},
            device_id_type=MESH,
        )
        for side, lon in ((0, right), (1, left))
    ]
    for copy in edge_copies + stat_copies:
        copy.start()

    for k in range(OWN):
        field[k, LAT : LAT + CELLS, :CHANS] = lat_ref[k].astype(F32).reshape(CELLS, CHANS)
    act[...] = silu(field[...])

    span = CELLS + LAT
    for g in range(SETS):
        parts = None
        for r in range(PACK):
            k = PACK * g + r
            sides = [act[k, LAT * b : LAT * b + span, :].astype(BF16) for b in range(3)]
            sides.append(field[k, LAT : LAT + span, :].astype(BF16))
            part = dot(jnp.concatenate(sides, axis=1), taps[r])
            parts = part if parts is None else parts + part
        summed = combine(parts) + bias
        total[g, :span] = summed
        total[g, span:] = jnp.zeros((BAND - span, WIDE), F32)
        for h in range(2):
            halves[2 * g + h] = total[g, :, h * LANES : (h + 1) * LANES]

    for i in range(LAT):
        for half in range(2 * SETS):
            rows_out[i, :, half * LANES : (half + 1) * LANES] = halves[
                half, pl.ds(i, SLOT, stride=LAT), :
            ].astype(BF16)
    states[m] = rows_out[m]

    def row_copy(to, source):
        return pltpu.make_async_remote_copy(
            src_ref=rows_out.at[to],
            dst_ref=states.at[source],
            send_sem=state_sent.at[to],
            recv_sem=state_got.at[source],
            device_id={"mem": to},
            device_id_type=MESH,
        )

    def end_copy(to, source):
        return pltpu.make_async_remote_copy(
            src_ref=ends_out.at[to],
            dst_ref=edges.at[source],
            send_sem=end_sent.at[to],
            recv_sem=end_got.at[source],
            device_id={"mem": to},
            device_id_type=MESH,
        )

    for step in range(1, MEM):
        row_copy(lax.rem(m + step, MEM), m).start()

    for side, copy in enumerate(edge_copies):
        copy.wait_recv()
        turn = silu(edge_in[side].astype(F32)).astype(BF16).astype(F32)
        parts = None
        for r in range(PACK):
            pick = [turn[(PACK * g + r) * LAT : (PACK * g + r + 1) * LAT] for g in range(SETS)]
            tap = 2 * side
            part = dot(
                jnp.concatenate(pick, axis=0).astype(BF16), taps[r, tap * LANES : (tap + 1) * LANES]
            )
            parts = part if parts is None else parts + part
        extra = combine(parts)
        first = 0 if side == 0 else CELLS - LAT
        for g in range(SETS):
            total[g, first : first + LAT] += extra[g * LAT : (g + 1) * LAT]
            for h in range(2):
                ends[pl.ds(4 * g + 2 * h + side, LAT, stride=16), :] = total[
                    g, first : first + LAT, h * LANES : (h + 1) * LANES
                ]
    ends_out[...] = ends[...].astype(BF16).reshape(LAT, 16, LANES)
    edges[m] = ends_out[m]
    for g in range(SETS):
        turned[g * WIDE : (g + 1) * WIDE] = total[g].T.astype(BF16)

    place = lax.broadcasted_iota(jnp.int32, (BAND, LANES), 0)
    channel = lax.broadcasted_iota(jnp.int32, (WIDE, WIDE), 0)

    def choose(pair, carry):
        first = cellp[pl.ds(2 * pair, 1), :]
        second = cellp[pl.ds(2 * pair + 1, 1), :]
        hot = jnp.concatenate(
            [
                jnp.where(place == first, 1.0, 0.0).astype(BF16),
                jnp.where(place == second, 1.0, 0.0).astype(BF16),
            ],
            axis=1,
        )
        chans = jnp.concatenate(
            [cellc[pl.ds(2 * pair, 1), :], cellc[pl.ds(2 * pair + 1, 1), :]], axis=1
        )
        for g in range(SETS):
            cells = dot(turned[g * WIDE : (g + 1) * WIDE, :], hot)
            for r in range(PACK):
                low, high = CHANS * r // 8 * 8, -(-CHANS * (r + 1) // 8) * 8
                mask = channel[low:high] - CHANS * r == chans
                found = jnp.sum(jnp.where(mask, cells[low:high], 0.0), axis=0, keepdims=True)
                spot = (PACK * g + r) * 16 + 2 * pair
                own[pl.ds(spot, 1), :] = found[:, :LANES]
                own[pl.ds(spot + 1, 1), :] = found[:, LANES:]
        return carry

    lax.fori_loop(0, OBS // WIDE, choose, 0)
    blocks[1, m] = own[...].astype(BF16)

    def arrival(slot, block):
        return pltpu.make_async_remote_copy(
            src_ref=blocks.at[1, block],
            dst_ref=blocks.at[slot, block],
            send_sem=sib_sent.at[block],
            recv_sem=block_got.at[slot, block],
            device_id={"lon": inner},
            device_id_type=MESH,
        )

    def along(block, sent, to):
        return pltpu.make_async_remote_copy(
            src_ref=blocks.at[1, block],
            dst_ref=blocks.at[1, block],
            send_sem=mate_sent.at[sent],
            recv_sem=block_got.at[1, block],
            device_id={"mem": to},
            device_id_type=MESH,
        )

    def across(block):
        return pltpu.make_async_remote_copy(
            src_ref=blocks.at[1, block],
            dst_ref=blocks.at[mine, block],
            send_sem=sib_sent.at[block],
            recv_sem=block_got.at[mine, block],
            device_id={"lon": inner},
            device_id_type=MESH,
        )

    def outward(block, sent, to):
        return pltpu.make_async_remote_copy(
            src_ref=blocks.at[1, block],
            dst_ref=blocks.at[theirs, block],
            send_sem=outer_sent.at[sent],
            recv_sem=block_got.at[theirs, block],
            device_id={"mem": to, "lon": outer},
            device_id_type=MESH,
        )

    half = m // 4 * 4
    partner = lax.rem(m + 4, MEM)
    partner_half = 4 - half
    mates = [half + lax.rem(m + step, 4) for step in range(1, 4)]
    partner_mates = [partner_half + lax.rem(m + step, 4) for step in range(1, 4)]

    @pl.when(far)
    def _():
        for step in range(MEM):
            to = lax.rem(m + step, MEM)
            outward(m, to, to).start()

    def pass_on(block):
        across(block).start()

        @pl.when(jnp.logical_not(far))
        def _():
            outward(block, block, m).start()

    along(m, 3, partner).start()
    for n in range(3):
        along(m, n, mates[n]).start()
    pass_on(m)
    for step in range(1, MEM):
        end_copy(lax.rem(m + step, MEM), m).start()
    for n in range(3):
        arrival(1, mates[n]).wait_recv()
        pass_on(mates[n])
    arrival(1, partner).wait_recv()
    for n in range(3):
        along(partner, 4 + n, mates[n]).start()
    pass_on(partner)
    for n in range(3):
        arrival(1, partner_mates[n]).wait_recv()
        pass_on(partner_mates[n])

    for block in range(MEM):
        arrival(mine, block).wait_recv()
        arrival(theirs, block).wait_recv()
    for copy in stat_copies:
        copy.wait()
    for copy in edge_copies:
        copy.wait_send()
    for block in range(MEM):
        across(block).wait_send()
        outward(block, block, m).wait_send()
    along(m, 3, partner).wait_send()
    for n in range(3):
        along(m, n, mates[n]).wait_send()
        along(partner, 4 + n, mates[n]).wait_send()
    for step in range(1, MEM):
        other = lax.rem(m + step, MEM)
        row_copy(other, other).wait_recv()
        row_copy(other, other).wait_send()
        end_copy(other, other).wait_recv()
        end_copy(other, other).wait_send()


def exchange(lat, weights, bias, cell, value, weight):
    vmem = pl.BlockSpec(memory_space=pltpu.VMEM)
    hbm = pl.BlockSpec(memory_space=pltpu.HBM)
    dma = pltpu.SemaphoreType.DMA
    return pl.pallas_call(
        exchange_kernel,
        out_shape=[
            jax.ShapeDtypeStruct((3, MEM, OWN * 16, LANES), BF16),
            jax.ShapeDtypeStruct((3, 2, 16, LANES), F32),
            jax.ShapeDtypeStruct((MEM, SLOT, SETS * WIDE), BF16),
            jax.ShapeDtypeStruct((MEM, 16, LANES), BF16),
        ],
        in_specs=[hbm] * 6,
        out_specs=[vmem] * 4,
        scratch_shapes=[
            pltpu.VMEM(lat.shape, BF16),
            pltpu.VMEM(weights.shape, BF16),
            pltpu.VMEM(bias.shape, F32),
            pltpu.VMEM(cell.shape, jnp.int32),
            pltpu.VMEM((OWN, BAND, LANES), F32),
            pltpu.VMEM((OWN, BAND, LANES), F32),
            pltpu.VMEM((LANES, LANES), F32),
            pltpu.VMEM((PACK, 4 * LANES, 3 * WIDE), BF16),
            pltpu.VMEM((SETS, BAND, WIDE), F32),
            pltpu.VMEM((2 * SETS, BAND, LANES), F32),
            pltpu.VMEM((SETS * WIDE, BAND), BF16),
            pltpu.VMEM((16, LANES), jnp.int32),
            pltpu.VMEM((16, LANES), jnp.int32),
            pltpu.VMEM((OWN * 16, LANES), F32),
            pltpu.VMEM((2, OWN * LAT, LANES), BF16),
            pltpu.VMEM((2, OWN * LAT, LANES), BF16),
            pltpu.VMEM((LAT, SLOT, SETS * WIDE), BF16),
            pltpu.VMEM((LAT * 16, LANES), F32),
            pltpu.VMEM((LAT, 16, LANES), BF16),
            dma((6,)),
            dma((2,)),
            dma((2,)),
            dma((2,)),
            dma((2,)),
            dma((7,)),
            dma((MEM,)),
            dma((MEM,)),
            dma((3, MEM)),
            dma((MEM,)),
            dma((MEM,)),
            dma((MEM,)),
            dma((MEM,)),
        ],
        compiler_params=pltpu.CompilerParams(
            collective_id=0, has_side_effects=True, vmem_limit_bytes=48 * 2**20
        ),
    )(lat, weights, bias, cell, value, weight)


def spread(piece):
    return jnp.concatenate([piece] * GROUP + [jnp.zeros((16, WIDE), BF16)], axis=0)


def analysis_kernel(
    list_ref, blocks, stats, states, edges, out,
    flat, table, picked, placing, stage, columns, diagonal, unpack, done,
):
    row = lax.broadcasted_iota(jnp.int32, (WIDE, WIDE), 0)
    col = lax.broadcasted_iota(jnp.int32, (WIDE, WIDE), 1)
    mask = jnp.zeros((WIDE, WIDE), F32)
    for s in range(GROUP):
        low, high = s * MEMBERS, (s + 1) * MEMBERS
        mask = jnp.where((row >= low) & (row < high) & (col >= low) & (col < high), 1.0, mask)
    diagonal[...] = mask.astype(BF16)
    row = lax.broadcasted_iota(jnp.int32, (WIDE, LANES), 0)
    col = lax.broadcasted_iota(jnp.int32, (WIDE, LANES), 1)
    for r in range(PACK):
        unpack[:, r * LANES : (r + 1) * LANES] = jnp.where(
            (row - CHANS * r == col) & (col < CHANS), 1.0, 0.0
        ).astype(BF16)
    row = lax.broadcasted_iota(jnp.int32, (LANES, WIDE), 0)
    col = lax.broadcasted_iota(jnp.int32, (LANES, WIDE), 1)
    member = row < MEMBERS
    for s in range(GROUP):
        inside = (col >= s * MEMBERS) & (col < (s + 1) * MEMBERS)
        kinds = (
            member & (col - s * MEMBERS == row),
            member & inside,
            ((row == MEMBERS) | (row == MEMBERS + 2)) & inside,
            ((row == MEMBERS + 1) | (row == MEMBERS + 3)) & inside,
        )
        for n, kind in enumerate(kinds):
            placing[s * LANES : (s + 1) * LANES, n * WIDE : (n + 1) * WIDE] = jnp.where(
                kind, 1.0, 0.0
            ).astype(BF16)

    for s in range(3):
        flat[s * MEM * OWN * 16 : (s + 1) * MEM * OWN * 16] = (
            blocks[s].astype(F32).reshape(MEM * OWN * 16, LANES)
        )
    blank = jnp.zeros((LANES - MEMBERS - 4, LANES), F32)

    def turn(k, carry):
        for s in range(3):
            cells = flat[pl.ds(s * MEM * OWN * 16 + k, MEMBERS, stride=16), :]
            extra = [stats[s, kind, pl.ds(k, 1), :] for kind in range(2)]
            high = [v.astype(BF16).astype(F32) for v in extra]
            low = [v - h for v, h in zip(extra, high)]
            whole = jnp.concatenate([cells] + high + low + [blank], axis=0)
            start = pl.multiple_of(s * OBS + k * LANES, LANES)
            table[pl.ds(start, LANES), :] = whole.T
        return carry

    lax.fori_loop(0, 16, turn, 0)

    for source in range(MEM):
        for g in range(SETS):
            parts = dot(states[source, :, g * WIDE : (g + 1) * WIDE], unpack[...])
            for r in range(PACK):
                columns[pl.ds(source * OWN + g * PACK + r, SLOT, stride=MEMBERS), :] = parts[
                    :, r * LANES : (r + 1) * LANES
                ]
    ends = edges[...].astype(F32)
    for g in range(SETS):
        sides = [
            jnp.concatenate([ends[:, 4 * g + side, :], ends[:, 4 * g + 2 + side, :]], axis=1)
            for side in range(2)
        ]
        parts = dot(jnp.concatenate(sides, axis=0).astype(BF16), unpack[...])
        for side, column in ((0, 0), (1, WIDTH - 1)):
            for r in range(PACK):
                columns[pl.ds(column * MEMBERS + g * PACK + r, MEM, stride=OWN), :] = parts[
                    side * MEM : (side + 1) * MEM, r * LANES : (r + 1) * LANES
                ]

    def gather(q, carry):
        base = q * OBS_COL
        for s in range(GROUP):
            for o in range(OBS_COL):
                index = list_ref[q * GROUP + s, 0, o]
                picked[s, pl.ds(base + o, 1), :] = table[pl.ds(index, 1), :]
        return carry

    lax.fori_loop(0, GROUPS, gather, 0)
    found = jnp.concatenate([picked[s].astype(BF16) for s in range(GROUP)], axis=1)
    stage[...] = dot(found, placing[...])

    eye = jnp.zeros((MEMBERS, WIDE), F32)
    row48 = lax.broadcasted_iota(jnp.int32, (MEMBERS, WIDE), 0)
    col48 = lax.broadcasted_iota(jnp.int32, (MEMBERS, WIDE), 1)
    for s in range(GROUP):
        eye = jnp.where(col48 - MEMBERS * s == row48, 1.0, eye)
    lane = lax.broadcasted_iota(jnp.int32, (1, WIDE), 1)
    block48 = [(lane >= s * MEMBERS) & (lane < (s + 1) * MEMBERS) for s in range(GROUP)]
    every = range(GROUPS)

    def block_sum(pieces):
        return dot(jnp.concatenate(pieces, axis=0), diagonal[...])

    grams, proj, traces = [], [], []
    for q in every:
        rows = slice(q * OBS_COL, (q + 1) * OBS_COL)
        mean = stage[rows, WIDE : 2 * WIDE] * (1.0 / MEMBERS)
        pert = stage[rows, :WIDE] - mean
        depart = stage[rows, 2 * WIDE : 3 * WIDE] - mean
        scaled = pert * stage[rows, 3 * WIDE :]
        proj.append(jnp.sum(scaled * depart, axis=0, keepdims=True))
        traces.append(jnp.sum(scaled * pert, axis=0, keepdims=True))
        high, low = split(pert)
        scaled_high, scaled_low = split(scaled)
        square = lax.dot_general(
            jnp.concatenate([scaled_high, scaled_low, scaled_high], axis=0),
            jnp.concatenate([high, high, low], axis=0),
            (((0,), (0,)), ((), ())),
            preferred_element_type=F32,
        )
        gram = (MEMBERS - 1.0) * eye
        for s in range(GROUP):
            piece = square[s * MEMBERS : (s + 1) * MEMBERS]
            gram = gram + jnp.where(block48[s], piece, 0.0)
        grams.append(gram)
    trace = jnp.concatenate(traces + [jnp.zeros((16 - GROUPS, WIDE), F32)], axis=0)
    one = trace.astype(BF16)
    two, three = split(trace - one.astype(F32))
    sums = block_sum([one, two, three])
    scales = MEMBERS * (MEMBERS - 1.0) + sums[:16] + sums[16:32] + sums[32:]
    invert, reroot = 1.0 / scales, lax.rsqrt(scales)

    def times(parts, high, low):
        count = len(parts)
        first = dot(jnp.concatenate([x for pair in parts for x in pair], axis=0), high)
        second = dot(jnp.concatenate([pair[0] for pair in parts], axis=0), low)
        size = parts[0][0].shape[0]
        return [
            first[2 * n * size : (2 * n + 1) * size]
            + first[(2 * n + 1) * size : (2 * n + 2) * size]
            + second[n * size : (n + 1) * size]
            for n in range(count)
        ]

    def lay(pair):
        return [spread(piece) * diagonal[...] for piece in pair]

    ratio = [grams[q] * invert[q : q + 1] for q in every]
    inverse = [None] * GROUPS
    for sweep in range(SWEEPS):
        factor = [1.5 * eye - 0.5 * r for r in ratio]
        weights = [lay(split(f)) for f in factor]
        products = []
        for q in every:
            todo = []
            if sweep < SWEEPS - 1:
                todo.append(split(ratio[q]))
            if sweep > 0:
                todo.append(split(inverse[q]))
            products.append(times(todo, *weights[q]))
        inverse = [products[q][-1] if sweep > 0 else factor[q] for q in every]
        if sweep < SWEEPS - 1:
            ratio = [times([split(products[q][0])], *weights[q])[0] for q in every]

    root = [inverse[q] * reroot[q : q + 1] for q in every]
    weights = [lay(split(r)) for r in root]
    vector = proj
    spot = lax.broadcasted_iota(jnp.int32, (16, WIDE), 0)
    for _ in range(2):
        rows = []
        for q in every:
            high = vector[q].astype(BF16).astype(F32)
            low = vector[q] - high
            rows.append(jnp.where(spot == 0, high, jnp.where(spot == 1, low, 0.0)).astype(BF16))
        first = [dot(rows[q], weights[q][0]) for q in every]
        second = [dot(rows[q], weights[q][1]) for q in every]
        vector = [first[q][0:1] + first[q][1:2] + second[q][0:1] for q in every]
    transform = [(MEMBERS - 1.0) ** 0.5 * root[q] + vector[q] for q in every]
    sums = block_sum([piece for t in transform for piece in split(t)])
    pieces = []
    for q in every:
        at = 2 * q * MEMBERS
        both = sums[at : at + MEMBERS] + sums[at + MEMBERS : at + 2 * MEMBERS]
        pieces.append(lay(split(transform[q] + (1.0 - both) * (1.0 / MEMBERS))))
    for q in every:
        field = columns[q * GROUP * MEMBERS : q * GROUP * MEMBERS + WIDE, :].astype(BF16)
        result = dot(pieces[q][0], field) + dot(pieces[q][1], field)
        for s in range(GROUP):
            done[pl.ds(q * GROUP + s, MEMBERS, stride=WIDTH), :] = result[
                s * MEMBERS : (s + 1) * MEMBERS
            ]
    out[...] = done[:, :CHANS]


def analysis(lists, blocks, stats, states, edges):
    vmem = pl.BlockSpec(memory_space=pltpu.VMEM)
    return pl.pallas_call(
        analysis_kernel,
        out_shape=jax.ShapeDtypeStruct((MEMBERS * WIDTH, CHANS), F32),
        in_specs=[pl.BlockSpec(memory_space=pltpu.SMEM)] + [vmem] * 4,
        out_specs=vmem,
        scratch_shapes=[
            pltpu.VMEM((3 * MEM * OWN * 16, LANES), F32),
            pltpu.VMEM((3 * OBS, LANES), F32),
            pltpu.VMEM((GROUP, GROUPS * OBS_COL, LANES), F32),
            pltpu.VMEM((GROUP * LANES, 4 * WIDE), BF16),
            pltpu.VMEM((GROUPS * OBS_COL, 4 * WIDE), F32),
            pltpu.VMEM((SLOT * MEMBERS, LANES), F32),
            pltpu.VMEM((WIDE, WIDE), BF16),
            pltpu.VMEM((WIDE, PACK * LANES), BF16),
            pltpu.VMEM((MEMBERS * WIDTH, LANES), F32),
        ],
        compiler_params=pltpu.CompilerParams(vmem_limit_bytes=48 * 2**20),
    )(lists, blocks, stats, states, edges)


def local(latent, conv_weight, conv_bias, obs_cell, obs_value, obs_weight, obs_list):
    blocks, stats, states, edges = exchange(
        jnp.transpose(latent, (0, 2, 1, 3)),
        conv_weight,
        conv_bias.reshape(1, CHANS),
        obs_cell.reshape(16, LANES),
        obs_value.reshape(16, LANES),
        obs_weight.reshape(16, LANES),
    )
    result = analysis(obs_list.reshape(WIDTH, 1, OBS_COL), blocks, stats, states, edges)
    return jnp.transpose(result.reshape(MEMBERS, WIDTH, 1, CHANS), (0, 2, 1, 3))


def solution(mesh):
    placed = (
        P("mem", None, "lon", None),
        P(),
        P(),
        P("lon"),
        P("lon"),
        P("lon"),
        P("mem", "lon", None),
    )
    return jax.shard_map(
        local, mesh=mesh, in_specs=placed, out_specs=P(None, "mem", "lon", None), check_vma=False
    )
```

time: 96.1 us -> 68.9 us (0.72)
  the two profiles are of different devices: /device:TPU:224 before, /device:TPU:1 now
where the time goes in v1:
time: 68.9 us; the launch traced here: 68.5 us
  Pallas kernels  63 us (91%)
  local copies, waits for them, and re-layouts  5.45 us (8%)
    pallas_call x1, Pallas kernels, exchange(): pl.pallas_call(exchange_kernel, out_shape=[jax.ShapeDtypeStruct((3, MEM,...  48.1 us
    pallas_call x1, Pallas kernels, analysis(): pl.pallas_call(analysis_kernel, out_shape=jax.ShapeDtypeStruct((MEMBERS *...  14.9 us
    unnamed x14, local copies, waits for them, and re-layouts  5.45 us

profile of v1, /device:TPU:1, one launch (start us, length us, event | category | flops | bytes accessed | tf_op | source)
XLA Modules:
  0.0 68.5 jit_solution(4443753579872313922)
XLA Ops:
  0.0 0.0 copy-start
  0.0 1.0 %copy-done = bf16[6,8,45,78]{3,1,2,0:T(8,128)(2,1)S(1)} copy-done((bf16[6,8,45,78]{3,1,2,0:T(8,128)(2,1)S(1)}, bf16[6,8,45,78]{3,1,2,0:T(8,128)(2,1)}, u32[]{:S(2)}) %copy-start) | copy-done | bytes 336984
  1.1 0.0 copy-start.1
  1.1 0.9 %copy-done.1 = bf16[3,3,78,78]{3,2,1,0:T(8,128)(2,1)S(1)} copy-done((bf16[3,3,78,78]{3,2,1,0:T(8,128)(2,1)S(1)}, bf16[3,3,78,78]{3,2,1,0:T(8,128)(2,1)}, u32[]{:S(2)}) %copy-start.1) | copy-done | bytes 109536
  2.0 0.0 copy-start.3
  2.0 0.7 %copy-done.3 = s32[2048]{0:T(1024)S(1)} copy-done((s32[2048]{0:T(1024)S(1)}, s32[2048]{0:T(1024)}, u32[]{:S(2)}) %copy-start.3) | copy-done | bytes 8216
  2.7 0.0 copy-start.4
  2.7 0.7 %copy-done.4 = f32[2048]{0:T(1024)S(1)} copy-done((f32[2048]{0:T(1024)S(1)}, f32[2048]{0:T(1024)}, u32[]{:S(2)}) %copy-start.4) | copy-done | bytes 8216
  3.4 0.0 copy-start.5
  3.4 0.7 %copy-done.5 = f32[2048]{0:T(1024)S(1)} copy-done((f32[2048]{0:T(1024)S(1)}, f32[2048]{0:T(1024)}, u32[]{:S(2)}) %copy-start.5) | copy-done | bytes 8216
  4.1 0.0 copy-start.6
  4.1 0.7 copy-done.6
  4.7 48.1 %shard_map.73 = (bf16[3,8,96,128]{3,2,1,0:T(8,128)(2,1)S(1)}, f32[3,2,16,128]{3,2,1,0:T(8,128)S(1)}, bf16[8,48,512]{2,1,0:T(8,128)(2,1)S(1)}, bf16[8,16,128]{2,1,0:T(8,128)(2,1)S(1)}) custom-call(bf16[6,45,8,78]{3,2,1,0:T(8,128)(2,1)S(1)} %bitcast.7, bf16[3,3,78,78]{3,2,1,0:T(8,128)(2,1)S(1)} %copy-done.1, f32[1,78]{1,0:T(1,128)S(1)} %bitcast.12, ...), custom_call_target="tpu_custom_call" | custom-call | tf_op jit(solution)/shard_map/pallas_call | solution.py:374
  52.9 0.0 copy-start.2
  52.9 0.7 %copy-done.2 = s32[1,45,64]{2,0,1:T(1,128)S(1)} copy-done((s32[1,45,64]{2,0,1:T(1,128)S(1)}, s32[1,45,64]{2,0,1:T(1,128)}, u32[]{:S(2)}) %copy-start.2) | copy-done | bytes 11544
  53.6 14.9 %shard_map.74 = f32[2160,78]{1,0:T(8,128)} custom-call(s32[45,1,64]{2,1,0:T(1,128)S(1)} %bitcast.8, bf16[3,8,96,128]{3,2,1,0:T(8,128)(2,1)S(1)} %get-tuple-element.9.blocks, f32[3,2,16,128]{3,2,1,0:T(8,128)S(1)} %get-tuple-element.10.stats, bf16[8,48,512]{2,1,0:T(8,128)(2,1)S(1)} %get-tuple-element.11.states, bf16[8,16,128]{2,1,0:T(8,128)(2,1)S(1)} %get-tuple-element.12.edges), custom_call_target="tpu_custom_call" | custom-call | tf_op jit(solution)/shard_map/pallas_call | solution.py:617
Async XLA Ops:
  0.0 1.1 %copy-start = (bf16[6,8,45,78]{3,1,2,0:T(8,128)(2,1)S(1)}, bf16[6,8,45,78]{3,1,2,0:T(8,128)(2,1)}, u32[]{:S(2)}) copy-start(bf16[6,8,45,78]{3,1,2,0:T(8,128)(2,1)} %param.7) | copy-start | bytes 1010884
  1.1 0.9 %copy-start.1 = (bf16[3,3,78,78]{3,2,1,0:T(8,128)(2,1)S(1)}, bf16[3,3,78,78]{3,2,1,0:T(8,128)(2,1)}, u32[]{:S(2)}) copy-start(bf16[3,3,78,78]{3,2,1,0:T(8,128)(2,1)} %w_hbm.1) | copy-start | bytes 328540
  2.0 0.7 %copy-start.3 = (s32[2048]{0:T(1024)S(1)}, s32[2048]{0:T(1024)}, u32[]{:S(2)}) copy-start(s32[2048]{0:T(1024)} %param.10) | copy-start | bytes 24580
  2.7 0.7 %copy-start.4 = (f32[2048]{0:T(1024)S(1)}, f32[2048]{0:T(1024)}, u32[]{:S(2)}) copy-start(f32[2048]{0:T(1024)} %param.11) | copy-start | bytes 24580
  3.4 0.7 %copy-start.5 = (f32[2048]{0:T(1024)S(1)}, f32[2048]{0:T(1024)}, u32[]{:S(2)}) copy-start(f32[2048]{0:T(1024)} %param.12) | copy-start | bytes 24580
  4.1 0.7 copy-start.6
  52.9 0.7 %copy-start.2 = (s32[1,45,64]{2,0,1:T(1,128)S(1)}, s32[1,45,64]{2,0,1:T(1,128)}, u32[]{:S(2)}) copy-start(s32[1,45,64]{2,0,1:T(1,128)} %param.13) | copy-start | bytes 34564

commit v2 on v1

--- a/solution.py
+++ b/solution.py
@@ -54,11 +54,207 @@
     return total.reshape(rows, WIDE)
 
 
+def spread(piece):
+    return jnp.concatenate([piece] * GROUP + [jnp.zeros((16, WIDE), BF16)], axis=0)
+
+
+def build_constants(placing, diagonal, unpack):
+    row = lax.broadcasted_iota(jnp.int32, (WIDE, WIDE), 0)
+    col = lax.broadcasted_iota(jnp.int32, (WIDE, WIDE), 1)
+    mask = jnp.zeros((WIDE, WIDE), F32)
+    for s in range(GROUP):
+        low, high = s * MEMBERS, (s + 1) * MEMBERS
+        mask = jnp.where((row >= low) & (row < high) & (col >= low) & (col < high), 1.0, mask)
+    diagonal[...] = mask.astype(BF16)
+    row = lax.broadcasted_iota(jnp.int32, (WIDE, LANES), 0)
+    col = lax.broadcasted_iota(jnp.int32, (WIDE, LANES), 1)
+    for r in range(PACK):
+        unpack[:, r * LANES : (r + 1) * LANES] = jnp.where(
+            (row - CHANS * r == col) & (col < CHANS), 1.0, 0.0
+        ).astype(BF16)
+    row = lax.broadcasted_iota(jnp.int32, (LANES, WIDE), 0)
+    col = lax.broadcasted_iota(jnp.int32, (LANES, WIDE), 1)
+    member = row < MEMBERS
+    for s in range(GROUP):
+        inside = (col >= s * MEMBERS) & (col < (s + 1) * MEMBERS)
+        kinds = (
+            member & (col - s * MEMBERS == row),
+            member & inside,
+            ((row == MEMBERS) | (row == MEMBERS + 2)) & inside,
+            ((row == MEMBERS + 1) | (row == MEMBERS + 3)) & inside,
+        )
+        for n, kind in enumerate(kinds):
+            placing[s * LANES : (s + 1) * LANES, n * WIDE : (n + 1) * WIDE] = jnp.where(
+                kind, 1.0, 0.0
+            ).astype(BF16)
+
+
+def weigh(list_ref, blocks, stats, flat, table, picked, placing, stage, diagonal):
+    for s in range(3):
+        flat[s * MEM * OWN * 16 : (s + 1) * MEM * OWN * 16] = (
+            blocks[s].astype(F32).reshape(MEM * OWN * 16, LANES)
+        )
+    blank = jnp.zeros((LANES - MEMBERS - 4, LANES), F32)
+
+    def turn(k, carry):
+        for s in range(3):
+            cells = flat[pl.ds(s * MEM * OWN * 16 + k, MEMBERS, stride=16), :]
+            extra = [stats[s, kind, pl.ds(k, 1), :] for kind in range(2)]
+            high = [v.astype(BF16).astype(F32) for v in extra]
+            low = [v - h for v, h in zip(extra, high)]
+            whole = jnp.concatenate([cells] + high + low + [blank], axis=0)
+            start = pl.multiple_of(s * OBS + k * LANES, LANES)
+            table[pl.ds(start, LANES), :] = whole.T
+        return carry
+
+    lax.fori_loop(0, 16, turn, 0)
+
+    def gather(q, carry):
+        base = q * OBS_COL
+        for s in range(GROUP):
+            for o in range(OBS_COL):
+                index = list_ref[q * GROUP + s, 0, o]
+                picked[s, pl.ds(base + o, 1), :] = table[pl.ds(index, 1), :]
+        return carry
+
+    lax.fori_loop(0, GROUPS, gather, 0)
+    found = jnp.concatenate([picked[s].astype(BF16) for s in range(GROUP)], axis=1)
+    stage[...] = dot(found, placing[...])
+
+    eye = jnp.zeros((MEMBERS, WIDE), F32)
+    row48 = lax.broadcasted_iota(jnp.int32, (MEMBERS, WIDE), 0)
+    col48 = lax.broadcasted_iota(jnp.int32, (MEMBERS, WIDE), 1)
+    for s in range(GROUP):
+        eye = jnp.where(col48 - MEMBERS * s == row48, 1.0, eye)
+    lane = lax.broadcasted_iota(jnp.int32, (1, WIDE), 1)
+    block48 = [(lane >= s * MEMBERS) & (lane < (s + 1) * MEMBERS) for s in range(GROUP)]
+    every = range(GROUPS)
+
+    def block_sum(pieces):
+        return dot(jnp.concatenate(pieces, axis=0), diagonal[...])
+
+    grams, proj, traces = [], [], []
+    for q in every:
+        rows = slice(q * OBS_COL, (q + 1) * OBS_COL)
+        mean = stage[rows, WIDE : 2 * WIDE] * (1.0 / MEMBERS)
+        pert = stage[rows, :WIDE] - mean
+        depart = stage[rows, 2 * WIDE : 3 * WIDE] - mean
+        scaled = pert * stage[rows, 3 * WIDE :]
+        proj.append(jnp.sum(scaled * depart, axis=0, keepdims=True))
+        traces.append(jnp.sum(scaled * pert, axis=0, keepdims=True))
+        high, low = split(pert)
+        scaled_high, scaled_low = split(scaled)
+        square = lax.dot_general(
+            jnp.concatenate([scaled_high, scaled_low, scaled_high], axis=0),
+            jnp.concatenate([high, high, low], axis=0),
+            (((0,), (0,)), ((), ())),
+            preferred_element_type=F32,
+        )
+        gram = (MEMBERS - 1.0) * eye
+        for s in range(GROUP):
+            piece = square[s * MEMBERS : (s + 1) * MEMBERS]
+            gram = gram + jnp.where(block48[s], piece, 0.0)
+        grams.append(gram)
+    trace = jnp.concatenate(traces + [jnp.zeros((16 - GROUPS, WIDE), F32)], axis=0)
+    one = trace.astype(BF16)
+    two, three = split(trace - one.astype(F32))
+    sums = block_sum([one, two, three])
+    scales = MEMBERS * (MEMBERS - 1.0) + sums[:16] + sums[16:32] + sums[32:]
+    invert, reroot = 1.0 / scales, lax.rsqrt(scales)
+
+    def times(parts, high, low):
+        count = len(parts)
+        first = dot(jnp.concatenate([x for pair in parts for x in pair], axis=0), high)
+        second = dot(jnp.concatenate([pair[0] for pair in parts], axis=0), low)
+        size = parts[0][0].shape[0]
+        return [
+            first[2 * n * size : (2 * n + 1) * size]
+            + first[(2 * n + 1) * size : (2 * n + 2) * size]
+            + second[n * size : (n + 1) * size]
+            for n in range(count)
+        ]
+
+    def lay(pair):
+        return [spread(piece) * diagonal[...] for piece in pair]
+
+    ratio = [grams[q] * invert[q : q + 1] for q in every]
+    inverse = [None] * GROUPS
+    for sweep in range(SWEEPS):
+        factor = [1.5 * eye - 0.5 * r for r in ratio]
+        weights = [lay(split(f)) for f in factor]
+        products = []
+        for q in every:
+            todo = []
+            if sweep < SWEEPS - 1:
+                todo.append(split(ratio[q]))
+            if sweep > 0:
+                todo.append(split(inverse[q]))
+            products.append(times(todo, *weights[q]))
+        inverse = [products[q][-1] if sweep > 0 else factor[q] for q in every]
+        if sweep < SWEEPS - 1:
+            ratio = [times([split(products[q][0])], *weights[q])[0] for q in every]
+
+    root = [inverse[q] * reroot[q : q + 1] for q in every]
+    weights = [lay(split(r)) for r in root]
+    vector = proj
+    spot = lax.broadcasted_iota(jnp.int32, (16, WIDE), 0)
+    for _ in range(2):
+        rows = []
+        for q in every:
+            high = vector[q].astype(BF16).astype(F32)
+            low = vector[q] - high
+            rows.append(jnp.where(spot == 0, high, jnp.where(spot == 1, low, 0.0)).astype(BF16))
+        first = [dot(rows[q], weights[q][0]) for q in every]
+        second = [dot(rows[q], weights[q][1]) for q in every]
+        vector = [first[q][0:1] + first[q][1:2] + second[q][0:1] for q in every]
+    transform = [(MEMBERS - 1.0) ** 0.5 * root[q] + vector[q] for q in every]
+    sums = block_sum([piece for t in transform for piece in split(t)])
+    pieces = []
+    for q in every:
+        at = 2 * q * MEMBERS
+        both = sums[at : at + MEMBERS] + sums[at + MEMBERS : at + 2 * MEMBERS]
+        pieces.append(lay(split(transform[q] + (1.0 - both) * (1.0 / MEMBERS))))
+    return pieces
+
+
+def apply(pieces, states, edges, unpack, columns, done, out):
+    for source in range(MEM):
+        for g in range(SETS):
+            parts = dot(states[source, :, g * WIDE : (g + 1) * WIDE], unpack[...])
+            for r in range(PACK):
+                columns[pl.ds(source * OWN + g * PACK + r, SLOT, stride=MEMBERS), :] = parts[
+                    :, r * LANES : (r + 1) * LANES
+                ]
+    ends = edges[...].astype(F32)
+    for g in range(SETS):
+        sides = [
+            jnp.concatenate([ends[:, 4 * g + side, :], ends[:, 4 * g + 2 + side, :]], axis=1)
+            for side in range(2)
+        ]
+        parts = dot(jnp.concatenate(sides, axis=0).astype(BF16), unpack[...])
+        for side, column in ((0, 0), (1, WIDTH - 1)):
+            for r in range(PACK):
+                columns[pl.ds(column * MEMBERS + g * PACK + r, MEM, stride=OWN), :] = parts[
+                    side * MEM : (side + 1) * MEM, r * LANES : (r + 1) * LANES
+                ]
+
+    for q in range(GROUPS):
+        field = columns[q * GROUP * MEMBERS : q * GROUP * MEMBERS + WIDE, :].astype(BF16)
+        result = dot(pieces[q][0], field) + dot(pieces[q][1], field)
+        for s in range(GROUP):
+            done[pl.ds(q * GROUP + s, MEMBERS, stride=WIDTH), :] = result[
+                s * MEMBERS : (s + 1) * MEMBERS
+            ]
+    out[...] = done[:, :CHANS]
+
+
 def exchange_kernel(
-    lat_hbm, w_hbm, bias_hbm, cell_hbm, value_hbm, weight_hbm,
-    blocks, stats, states, edges,
-    lat_ref, w_ref, bias_ref, cell_ref, field, act, wpad, taps, total, halves, turned, cellp, cellc,
+    lat_hbm, w_hbm, bias_hbm, cell_hbm, value_hbm, weight_hbm, list_hbm,
+    out,
+    lat_ref, w_ref, bias_ref, cell_ref, list_ref, blocks, stats, states, edges,
+    field, act, wpad, taps, total, halves, turned, cellp, cellc,
     own, edge_out, edge_in, rows_out, ends, ends_out,
+    flat, table, picked, placing, stage, columns, diagonal, unpack, done,
     loaded, edge_sent, edge_got, stat_sent, stat_got, mate_sent, sib_sent, outer_sent, block_got,
     state_sent, state_got, end_sent, end_got,
 ):
@@ -97,6 +293,7 @@
                 (cell_hbm, cell_ref),
                 (value_hbm, stats.at[1, 0]),
                 (weight_hbm, stats.at[1, 1]),
+                (list_hbm, list_ref),
             )
         )
     ]
@@ -107,7 +304,8 @@
     field[...] = jnp.zeros_like(field)
     wpad[...] = jnp.zeros_like(wpad)
     ends[...] = jnp.zeros_like(ends)
-    for load in loads:
+    build_constants(placing, diagonal, unpack)
+    for load in loads[:-1]:
         load.wait()
     for side, column in ((0, WIDTH - 1), (1, 0)):
         edge = lat_ref[:, column].astype(F32).reshape(OWN * LAT, CHANS)
@@ -133,10 +331,10 @@
     bias = bias + pltpu.roll(bias, CHANS, 1) + pltpu.roll(bias, 2 * CHANS, 1)
     bias = jnp.where(lane[:8, :] < PACK * CHANS, bias, 0.0)[:1, :]
 
-    flat = cell_ref[...]
-    pixel = jnp.floor((flat.astype(F32) + 0.5) * (1.0 / CHANS)).astype(jnp.int32)
+    named = cell_ref[...]
+    pixel = jnp.floor((named.astype(F32) + 0.5) * (1.0 / CHANS)).astype(jnp.int32)
     row = jnp.floor((pixel.astype(F32) + 0.5) * (1.0 / WIDTH)).astype(jnp.int32)
-    cellc[...] = flat - CHANS * pixel
+    cellc[...] = named - CHANS * pixel
     cellp[...] = (pixel - WIDTH * row) * LAT + row
 
     pl.semaphore_wait(barrier, jnp.where(far, 2 * MEM, MEM + 1))
@@ -212,8 +410,6 @@
             device_id_type=MESH,
         )
 
-    for step in range(1, MEM):
-        row_copy(lax.rem(m + step, MEM), m).start()
 
     for side, copy in enumerate(edge_copies):
         copy.wait_recv()
@@ -345,11 +541,22 @@
         arrival(1, partner_mates[n]).wait_recv()
         pass_on(partner_mates[n])
 
+    for step in range(1, MEM):
+        row_copy(lax.rem(m + step, MEM), m).start()
     for block in range(MEM):
         arrival(mine, block).wait_recv()
         arrival(theirs, block).wait_recv()
     for copy in stat_copies:
         copy.wait()
+    loads[-1].wait()
+    pieces = weigh(list_ref, blocks, stats, flat, table, picked, placing, stage, diagonal)
+
+    for step in range(1, MEM):
+        other = lax.rem(m + step, MEM)
+        row_copy(other, other).wait_recv()
+        end_copy(other, other).wait_recv()
+    apply(pieces, states, edges, unpack, columns, done, out)
+
     for copy in edge_copies:
         copy.wait_send()
     for block in range(MEM):
@@ -361,31 +568,29 @@
         along(partner, 4 + n, mates[n]).wait_send()
     for step in range(1, MEM):
         other = lax.rem(m + step, MEM)
-        row_copy(other, other).wait_recv()
         row_copy(other, other).wait_send()
-        end_copy(other, other).wait_recv()
         end_copy(other, other).wait_send()
 
 
-def exchange(lat, weights, bias, cell, value, weight):
+def exchange(lat, weights, bias, cell, value, weight, lists):
+    hbm = pl.BlockSpec(memory_space=pltpu.HBM)
     vmem = pl.BlockSpec(memory_space=pltpu.VMEM)
-    hbm = pl.BlockSpec(memory_space=pltpu.HBM)
     dma = pltpu.SemaphoreType.DMA
     return pl.pallas_call(
         exchange_kernel,
-        out_shape=[
-            jax.ShapeDtypeStruct((3, MEM, OWN * 16, LANES), BF16),
-            jax.ShapeDtypeStruct((3, 2, 16, LANES), F32),
-            jax.ShapeDtypeStruct((MEM, SLOT, SETS * WIDE), BF16),
-            jax.ShapeDtypeStruct((MEM, 16, LANES), BF16),
-        ],
-        in_specs=[hbm] * 6,
-        out_specs=[vmem] * 4,
+        out_shape=jax.ShapeDtypeStruct((MEMBERS * WIDTH, CHANS), F32),
+        in_specs=[hbm] * 7,
+        out_specs=vmem,
         scratch_shapes=[
             pltpu.VMEM(lat.shape, BF16),
             pltpu.VMEM(weights.shape, BF16),
             pltpu.VMEM(bias.shape, F32),
             pltpu.VMEM(cell.shape, jnp.int32),
+            pltpu.SMEM(lists.shape, jnp.int32),
+            pltpu.VMEM((3, MEM, OWN * 16, LANES), BF16),
+            pltpu.VMEM((3, 2, 16, LANES), F32),
+            pltpu.VMEM((MEM, SLOT, SETS * WIDE), BF16),
+            pltpu.VMEM((MEM, 16, LANES), BF16),
             pltpu.VMEM((OWN, BAND, LANES), F32),
             pltpu.VMEM((OWN, BAND, LANES), F32),
             pltpu.VMEM((LANES, LANES), F32),
@@ -401,7 +606,16 @@
             pltpu.VMEM((LAT, SLOT, SETS * WIDE), BF16),
             pltpu.VMEM((LAT * 16, LANES), F32),
             pltpu.VMEM((LAT, 16, LANES), BF16),
-            dma((6,)),
+            pltpu.VMEM((3 * MEM * OWN * 16, LANES), F32),
+            pltpu.VMEM((3 * OBS, LANES), F32),
+            pltpu.VMEM((GROUP, GROUPS * OBS_COL, LANES), F32),
+            pltpu.VMEM((GROUP * LANES, 4 * WIDE), BF16),
+            pltpu.VMEM((GROUPS * OBS_COL, 4 * WIDE), F32),
+            pltpu.VMEM((SLOT * MEMBERS, LANES), F32),
+            pltpu.VMEM((WIDE, WIDE), BF16),
+            pltpu.VMEM((WIDE, PACK * LANES), BF16),
+            pltpu.VMEM((MEMBERS * WIDTH, LANES), F32),
+            dma((7,)),
             dma((2,)),
             dma((2,)),
             dma((2,)),
@@ -416,234 +630,21 @@
             dma((MEM,)),
         ],
         compiler_params=pltpu.CompilerParams(
-            collective_id=0, has_side_effects=True, vmem_limit_bytes=48 * 2**20
+            collective_id=0, has_side_effects=True, vmem_limit_bytes=60 * 2**20
         ),
-    )(lat, weights, bias, cell, value, weight)
-
-
-def spread(piece):
-    return jnp.concatenate([piece] * GROUP + [jnp.zeros((16, WIDE), BF16)], axis=0)
-
-
-def analysis_kernel(
-    list_ref, blocks, stats, states, edges, out,
-    flat, table, picked, placing, stage, columns, diagonal, unpack, done,
-):
-    row = lax.broadcasted_iota(jnp.int32, (WIDE, WIDE), 0)
-    col = lax.broadcasted_iota(jnp.int32, (WIDE, WIDE), 1)
-    mask = jnp.zeros((WIDE, WIDE), F32)
-    for s in range(GROUP):
-        low, high = s * MEMBERS, (s + 1) * MEMBERS
-        mask = jnp.where((row >= low) & (row < high) & (col >= low) & (col < high), 1.0, mask)
-    diagonal[...] = mask.astype(BF16)
-    row = lax.broadcasted_iota(jnp.int32, (WIDE, LANES), 0)
-    col = lax.broadcasted_iota(jnp.int32, (WIDE, LANES), 1)
-    for r in range(PACK):
-        unpack[:, r * LANES : (r + 1) * LANES] = jnp.where(
-            (row - CHANS * r == col) & (col < CHANS), 1.0, 0.0
-        ).astype(BF16)
-    row = lax.broadcasted_iota(jnp.int32, (LANES, WIDE), 0)
-    col = lax.broadcasted_iota(jnp.int32, (LANES, WIDE), 1)
-    member = row < MEMBERS
-    for s in range(GROUP):
-        inside = (col >= s * MEMBERS) & (col < (s + 1) * MEMBERS)
-        kinds = (
-            member & (col - s * MEMBERS == row),
-            member & inside,
-            ((row == MEMBERS) | (row == MEMBERS + 2)) & inside,
-            ((row == MEMBERS + 1) | (row == MEMBERS + 3)) & inside,
-        )
-        for n, kind in enumerate(kinds):
-            placing[s * LANES : (s + 1) * LANES, n * WIDE : (n + 1) * WIDE] = jnp.where(
-                kind, 1.0, 0.0
-            ).astype(BF16)
-
-    for s in range(3):
-        flat[s * MEM * OWN * 16 : (s + 1) * MEM * OWN * 16] = (
-            blocks[s].astype(F32).reshape(MEM * OWN * 16, LANES)
-        )
-    blank = jnp.zeros((LANES - MEMBERS - 4, LANES), F32)
-
-    def turn(k, carry):
-        for s in range(3):
-            cells = flat[pl.ds(s * MEM * OWN * 16 + k, MEMBERS, stride=16), :]
-            extra = [stats[s, kind, pl.ds(k, 1), :] for kind in range(2)]
-            high = [v.astype(BF16).astype(F32) for v in extra]
-            low = [v - h for v, h in zip(extra, high)]
-            whole = jnp.concatenate([cells] + high + low + [blank], axis=0)
-            start = pl.multiple_of(s * OBS + k * LANES, LANES)
-            table[pl.ds(start, LANES), :] = whole.T
-        return carry
-
-    lax.fori_loop(0, 16, turn, 0)
-
-    for source in range(MEM):
-        for g in range(SETS):
-            parts = dot(states[source, :, g * WIDE : (g + 1) * WIDE], unpack[...])
-            for r in range(PACK):
-                columns[pl.ds(source * OWN + g * PACK + r, SLOT, stride=MEMBERS), :] = parts[
-                    :, r * LANES : (r + 1) * LANES
-                ]
-    ends = edges[...].astype(F32)
-    for g in range(SETS):
-        sides = [
-            jnp.concatenate([ends[:, 4 * g + side, :], ends[:, 4 * g + 2 + side, :]], axis=1)
-            for side in range(2)
-        ]
-        parts = dot(jnp.concatenate(sides, axis=0).astype(BF16), unpack[...])
-        for side, column in ((0, 0), (1, WIDTH - 1)):
-            for r in range(PACK):
-                columns[pl.ds(column * MEMBERS + g * PACK + r, MEM, stride=OWN), :] = parts[
-                    side * MEM : (side + 1) * MEM, r * LANES : (r + 1) * LANES
-                ]
-
-    def gather(q, carry):
-        base = q * OBS_COL
-        for s in range(GROUP):
-            for o in range(OBS_COL):
-                index = list_ref[q * GROUP + s, 0, o]
-                picked[s, pl.ds(base + o, 1), :] = table[pl.ds(index, 1), :]
-        return carry
-
-    lax.fori_loop(0, GROUPS, gather, 0)
-    found = jnp.concatenate([picked[s].astype(BF16) for s in range(GROUP)], axis=1)
-    stage[...] = dot(found, placing[...])
-
-    eye = jnp.zeros((MEMBERS, WIDE), F32)
-    row48 = lax.broadcasted_iota(jnp.int32, (MEMBERS, WIDE), 0)
-    col48 = lax.broadcasted_iota(jnp.int32, (MEMBERS, WIDE), 1)
-    for s in range(GROUP):
-        eye = jnp.where(col48 - MEMBERS * s == row48, 1.0, eye)
-    lane = lax.broadcasted_iota(jnp.int32, (1, WIDE), 1)
-    block48 = [(lane >= s * MEMBERS) & (lane < (s + 1) * MEMBERS) for s in range(GROUP)]
-    every = range(GROUPS)
-
-    def block_sum(pieces):
-        return dot(jnp.concatenate(pieces, axis=0), diagonal[...])
-
-    grams, proj, traces = [], [], []
-    for q in every:
-        rows = slice(q * OBS_COL, (q + 1) * OBS_COL)
-        mean = stage[rows, WIDE : 2 * WIDE] * (1.0 / MEMBERS)
-        pert = stage[rows, :WIDE] - mean
-        depart = stage[rows, 2 * WIDE : 3 * WIDE] - mean
-        scaled = pert * stage[rows, 3 * WIDE :]
-        proj.append(jnp.sum(scaled * depart, axis=0, keepdims=True))
-        traces.append(jnp.sum(scaled * pert, axis=0, keepdims=True))
-        high, low = split(pert)
-        scaled_high, scaled_low = split(scaled)
-        square = lax.dot_general(
-            jnp.concatenate([scaled_high, scaled_low, scaled_high], axis=0),
-            jnp.concatenate([high, high, low], axis=0),
-            (((0,), (0,)), ((), ())),
-            preferred_element_type=F32,
-        )
-        gram = (MEMBERS - 1.0) * eye
-        for s in range(GROUP):
-            piece = square[s * MEMBERS : (s + 1) * MEMBERS]
-            gram = gram + jnp.where(block48[s], piece, 0.0)
-        grams.append(gram)
-    trace = jnp.concatenate(traces + [jnp.zeros((16 - GROUPS, WIDE), F32)], axis=0)
-    one = trace.astype(BF16)
-    two, three = split(trace - one.astype(F32))
-    sums = block_sum([one, two, three])
-    scales = MEMBERS * (MEMBERS - 1.0) + sums[:16] + sums[16:32] + sums[32:]
-    invert, reroot = 1.0 / scales, lax.rsqrt(scales)
-
-    def times(parts, high, low):
-        count = len(parts)
-        first = dot(jnp.concatenate([x for pair in parts for x in pair], axis=0), high)
-        second = dot(jnp.concatenate([pair[0] for pair in parts], axis=0), low)
-        size = parts[0][0].shape[0]
-        return [
-            first[2 * n * size : (2 * n + 1) * size]
-            + first[(2 * n + 1) * size : (2 * n + 2) * size]
-            + second[n * size : (n + 1) * size]
-            for n in range(count)
-        ]
-
-    def lay(pair):
-        return [spread(piece) * diagonal[...] for piece in pair]
-
-    ratio = [grams[q] * invert[q : q + 1] for q in every]
-    inverse = [None] * GROUPS
-    for sweep in range(SWEEPS):
-        factor = [1.5 * eye - 0.5 * r for r in ratio]
-        weights = [lay(split(f)) for f in factor]
-        products = []
-        for q in every:
-            todo = []
-            if sweep < SWEEPS - 1:
-                todo.append(split(ratio[q]))
-            if sweep > 0:
-                todo.append(split(inverse[q]))
-            products.append(times(todo, *weights[q]))
-        inverse = [products[q][-1] if sweep > 0 else factor[q] for q in every]
-        if sweep < SWEEPS - 1:
-            ratio = [times([split(products[q][0])], *weights[q])[0] for q in every]
-
-    root = [inverse[q] * reroot[q : q + 1] for q in every]
-    weights = [lay(split(r)) for r in root]
-    vector = proj
-    spot = lax.broadcasted_iota(jnp.int32, (16, WIDE), 0)
-    for _ in range(2):
-        rows = []
-        for q in every:
-            high = vector[q].astype(BF16).astype(F32)
-            low = vector[q] - high
-            rows.append(jnp.where(spot == 0, high, jnp.where(spot == 1, low, 0.0)).astype(BF16))
-        first = [dot(rows[q], weights[q][0]) for q in every]
-        second = [dot(rows[q], weights[q][1]) for q in every]
-        vector = [first[q][0:1] + first[q][1:2] + second[q][0:1] for q in every]
-    transform = [(MEMBERS - 1.0) ** 0.5 * root[q] + vector[q] for q in every]
-    sums = block_sum([piece for t in transform for piece in split(t)])
-    pieces = []
-    for q in every:
-        at = 2 * q * MEMBERS
-        both = sums[at : at + MEMBERS] + sums[at + MEMBERS : at + 2 * MEMBERS]
-        pieces.append(lay(split(transform[q] + (1.0 - both) * (1.0 / MEMBERS))))
-    for q in every:
-        field = columns[q * GROUP * MEMBERS : q * GROUP * MEMBERS + WIDE, :].astype(BF16)
-        result = dot(pieces[q][0], field) + dot(pieces[q][1], field)
-        for s in range(GROUP):
-            done[pl.ds(q * GROUP + s, MEMBERS, stride=WIDTH), :] = result[
-                s * MEMBERS : (s + 1) * MEMBERS
-            ]
-    out[...] = done[:, :CHANS]
-
-
-def analysis(lists, blocks, stats, states, edges):
-    vmem = pl.BlockSpec(memory_space=pltpu.VMEM)
-    return pl.pallas_call(
-        analysis_kernel,
-        out_shape=jax.ShapeDtypeStruct((MEMBERS * WIDTH, CHANS), F32),
-        in_specs=[pl.BlockSpec(memory_space=pltpu.SMEM)] + [vmem] * 4,
-        out_specs=vmem,
-        scratch_shapes=[
-            pltpu.VMEM((3 * MEM * OWN * 16, LANES), F32),
-            pltpu.VMEM((3 * OBS, LANES), F32),
-            pltpu.VMEM((GROUP, GROUPS * OBS_COL, LANES), F32),
-            pltpu.VMEM((GROUP * LANES, 4 * WIDE), BF16),
-            pltpu.VMEM((GROUPS * OBS_COL, 4 * WIDE), F32),
-            pltpu.VMEM((SLOT * MEMBERS, LANES), F32),
-            pltpu.VMEM((WIDE, WIDE), BF16),
-            pltpu.VMEM((WIDE, PACK * LANES), BF16),
-            pltpu.VMEM((MEMBERS * WIDTH, LANES), F32),
-        ],
-        compiler_params=pltpu.CompilerParams(vmem_limit_bytes=48 * 2**20),
-    )(lists, blocks, stats, states, edges)
+    )(lat, weights, bias, cell, value, weight, lists)
 
 
 def local(latent, conv_weight, conv_bias, obs_cell, obs_value, obs_weight, obs_list):
-    blocks, stats, states, edges = exchange(
+    result = exchange(
         jnp.transpose(latent, (0, 2, 1, 3)),
         conv_weight,
         conv_bias.reshape(1, CHANS),
         obs_cell.reshape(16, LANES),
         obs_value.reshape(16, LANES),
         obs_weight.reshape(16, LANES),
+        obs_list.reshape(WIDTH, 1, OBS_COL),
     )
-    result = analysis(obs_list.reshape(WIDTH, 1, OBS_COL), blocks, stats, states, edges)
     return jnp.transpose(result.reshape(MEMBERS, WIDTH, 1, CHANS), (0, 2, 1, 3))
 
 

time: 68.9 us -> 65.9 us (0.956)
  local copies, waits for them, and re-layouts: 5.45 us -> 2.33 us
    unnamed x14 -> x1, local copies, waits for them, and re-layouts: 5.45 us -> 2.33 us
    pallas_call x2 -> x1, Pallas kernels: 63 us -> 63.4 us  [exchange(): pl.pallas_call(exchange_kernel, out_shape=jax.ShapeDtypeStruct((MEMBERS *...]
where the time goes in v2:
time: 65.9 us; the launch traced here: 65.8 us
  Pallas kernels  63.4 us (96%)
  local copies, waits for them, and re-layouts  2.33 us (4%)
    pallas_call x1, Pallas kernels, exchange(): pl.pallas_call(exchange_kernel, out_shape=jax.ShapeDtypeStruct((MEMBERS *...  63.4 us
    unnamed x1, local copies, waits for them, and re-layouts  2.33 us

profile of v2, /device:TPU:1, one launch (start us, length us, event | category | flops | bytes accessed | tf_op | source)
XLA Modules:
  0.0 65.8 jit_solution(9366596716102658048)
XLA Ops:
  0.0 63.4 %shard_map.73 = f32[2160,78]{1,0:T(8,128)} custom-call(bf16[6,45,8,78]{3,2,1,0:T(8,128)(2,1)} %bitcast.8, bf16[3,3,78,78]{3,2,1,0:T(8,128)(2,1)} %w_hbm.1, f32[1,78]{1,0:T(1,128)} %bitcast.13, s32[16,128]{1,0:T(8,128)} %bitcast.10, f32[16,128]{1,0:T(8,128)} %bitcast.11, f32[16,128]{1,0:T(8,128)} %bitcast.12, s32[45,1,64]{2,1,0:T(1,128)} %bitcast.9), custom_call_target="tpu_custom_call" | custom-call | tf_op jit(solution)/shard_map/pallas_call | solution.py:579
  63.4 2.3 %copy.11 = f32[48,1,45,78]{3,1,2,0:T(1,128)} copy(f32[48,1,45,78]{3,1,2,0:T(1,128)} %bitcast.7) | data formatting | bytes 1347840

commit v3 on v2

--- a/solution.py
+++ b/solution.py
@@ -25,6 +25,8 @@
 BAND = 384
 WIDE = 2 * LANES
 SLOT = 48
+EARLY = (3, 4, 5)
+LATE = (1, 2, 6, 7)
 F32 = jnp.float32
 BF16 = jnp.bfloat16
 MESH = pl.DeviceIdType.MESH
@@ -89,26 +91,24 @@
             ).astype(BF16)
 
 
-def weigh(list_ref, blocks, stats, flat, table, picked, placing, stage, diagonal):
-    for s in range(3):
-        flat[s * MEM * OWN * 16 : (s + 1) * MEM * OWN * 16] = (
-            blocks[s].astype(F32).reshape(MEM * OWN * 16, LANES)
-        )
+def fill(slot, blocks, stats, flat, table):
+    flat[...] = blocks[slot].astype(F32).reshape(MEM * OWN * 16, LANES)
     blank = jnp.zeros((LANES - MEMBERS - 4, LANES), F32)
 
     def turn(k, carry):
-        for s in range(3):
-            cells = flat[pl.ds(s * MEM * OWN * 16 + k, MEMBERS, stride=16), :]
-            extra = [stats[s, kind, pl.ds(k, 1), :] for kind in range(2)]
-            high = [v.astype(BF16).astype(F32) for v in extra]
-            low = [v - h for v, h in zip(extra, high)]
-            whole = jnp.concatenate([cells] + high + low + [blank], axis=0)
-            start = pl.multiple_of(s * OBS + k * LANES, LANES)
-            table[pl.ds(start, LANES), :] = whole.T
+        cells = flat[pl.ds(k, MEMBERS, stride=16), :]
+        extra = [stats[slot, kind, pl.ds(k, 1), :] for kind in range(2)]
+        high = [v.astype(BF16).astype(F32) for v in extra]
+        low = [v - h for v, h in zip(extra, high)]
+        whole = jnp.concatenate([cells] + high + low + [blank], axis=0)
+        start = pl.multiple_of(slot * OBS + k * LANES, LANES)
+        table[pl.ds(start, LANES), :] = whole.T
         return carry
 
-    lax.fori_loop(0, 16, turn, 0)
-
+    lax.fori_loop(0, 16, turn, 0, unroll=8)
+
+
+def weigh(list_ref, table, picked, placing, stage, diagonal):
     def gather(q, carry):
         base = q * OBS_COL
         for s in range(GROUP):
@@ -252,7 +252,7 @@
     lat_hbm, w_hbm, bias_hbm, cell_hbm, value_hbm, weight_hbm, list_hbm,
     out,
     lat_ref, w_ref, bias_ref, cell_ref, list_ref, blocks, stats, states, edges,
-    field, act, wpad, taps, total, halves, turned, cellp, cellc,
+    field, act, wpad, taps, total, halves, turned, turned_rim, cellp, cellc,
     own, edge_out, edge_in, rows_out, ends, ends_out,
     flat, table, picked, placing, stage, columns, diagonal, unpack, done,
     loaded, edge_sent, edge_got, stat_sent, stat_got, mate_sent, sib_sent, outer_sent, block_got,
@@ -269,6 +269,9 @@
     mine, theirs = 2 * core, 2 - 2 * core
     far = lax.rem(jnp.where(core == 0, t, t + 1), tiles // 2) == 0
 
+    quarter, pair = tiles // 4, lax.rem(t // 2, tiles // 4)
+    busy = (pair == 0) | (pair == quarter - 1)
+
     barrier = pltpu.get_barrier_semaphore()
     for lon in (left, right):
         pl.semaphore_signal(barrier, inc=1, device_id={"lon": lon}, device_id_type=MESH)
@@ -304,13 +307,17 @@
     field[...] = jnp.zeros_like(field)
     wpad[...] = jnp.zeros_like(wpad)
     ends[...] = jnp.zeros_like(ends)
-    build_constants(placing, diagonal, unpack)
-    for load in loads[:-1]:
-        load.wait()
+    loads[0].wait()
     for side, column in ((0, WIDTH - 1), (1, 0)):
         edge = lat_ref[:, column].astype(F32).reshape(OWN * LAT, CHANS)
         edge_out[side, :, :CHANS] = edge.astype(BF16)
 
+    for k in range(OWN):
+        field[k, LAT : LAT + CELLS, :CHANS] = lat_ref[k].astype(F32).reshape(CELLS, CHANS)
+    act[...] = silu(field[...])
+
+    for load in loads[1:-1]:
+        load.wait()
     lane = lax.broadcasted_iota(jnp.int32, (LANES, WIDE), 1)
     depth = lax.broadcasted_iota(jnp.int32, (LANES, WIDE), 0)
     blank = jnp.zeros((LANES, LANES), F32)
@@ -331,43 +338,6 @@
     bias = bias + pltpu.roll(bias, CHANS, 1) + pltpu.roll(bias, 2 * CHANS, 1)
     bias = jnp.where(lane[:8, :] < PACK * CHANS, bias, 0.0)[:1, :]
 
-    named = cell_ref[...]
-    pixel = jnp.floor((named.astype(F32) + 0.5) * (1.0 / CHANS)).astype(jnp.int32)
-    row = jnp.floor((pixel.astype(F32) + 0.5) * (1.0 / WIDTH)).astype(jnp.int32)
-    cellc[...] = named - CHANS * pixel
-    cellp[...] = (pixel - WIDTH * row) * LAT + row
-
-    pl.semaphore_wait(barrier, jnp.where(far, 2 * MEM, MEM + 1))
-
-    edge_copies = [
-        pltpu.make_async_remote_copy(
-            src_ref=edge_out.at[side],
-            dst_ref=edge_in.at[side],
-            send_sem=edge_sent.at[side],
-            recv_sem=edge_got.at[side],
-            device_id={"lon": lon},
-            device_id_type=MESH,
-        )
-        for side, lon in ((0, right), (1, left))
-    ]
-    stat_copies = [
-        pltpu.make_async_remote_copy(
-            src_ref=stats.at[1],
-            dst_ref=stats.at[2 * side],
-            send_sem=stat_sent.at[side],
-            recv_sem=stat_got.at[side],
-            device_id={"lon": lon},
-            device_id_type=MESH,
-        )
-        for side, lon in ((0, right), (1, left))
-    ]
-    for copy in edge_copies + stat_copies:
-        copy.start()
-
-    for k in range(OWN):
-        field[k, LAT : LAT + CELLS, :CHANS] = lat_ref[k].astype(F32).reshape(CELLS, CHANS)
-    act[...] = silu(field[...])
-
     span = CELLS + LAT
     for g in range(SETS):
         parts = None
@@ -383,6 +353,66 @@
         for h in range(2):
             halves[2 * g + h] = total[g, :, h * LANES : (h + 1) * LANES]
 
+    named = cell_ref[...]
+    pixel = jnp.floor((named.astype(F32) + 0.5) * (1.0 / CHANS)).astype(jnp.int32)
+    row = jnp.floor((pixel.astype(F32) + 0.5) * (1.0 / WIDTH)).astype(jnp.int32)
+    cellc[...] = named - CHANS * pixel
+    cellp[...] = (pixel - WIDTH * row) * LAT + row
+
+    pl.semaphore_wait(barrier, jnp.where(far, 2 * MEM, MEM + 1))
+
+    edge_copies = [
+        pltpu.make_async_remote_copy(
+            src_ref=edge_out.at[side],
+            dst_ref=edge_in.at[side],
+            send_sem=edge_sent.at[side],
+            recv_sem=edge_got.at[side],
+            device_id={"lon": lon},
+            device_id_type=MESH,
+        )
+        for side, lon in ((0, right), (1, left))
+    ]
+    stat_copies = [
+        pltpu.make_async_remote_copy(
+            src_ref=stats.at[1],
+            dst_ref=stats.at[2 * side],
+            send_sem=stat_sent.at[side],
+            recv_sem=stat_got.at[side],
+            device_id={"lon": lon},
+            device_id_type=MESH,
+        )
+        for side, lon in ((0, right), (1, left))
+    ]
+    for copy in edge_copies:
+        copy.start()
+
+
+    def mend(side):
+        pltpu.make_async_remote_copy(
+            src_ref=edge_out.at[side],
+            dst_ref=edge_in.at[side],
+            send_sem=edge_sent.at[side],
+            recv_sem=edge_got.at[side],
+            device_id={"lon": inner},
+            device_id_type=MESH,
+        ).wait_recv()
+        turn = silu(edge_in[side].astype(F32)).astype(BF16).astype(F32)
+        tap = pl.multiple_of(2 * side * LANES, LANES)
+        parts = None
+        for r in range(PACK):
+            pick = [turn[(PACK * g + r) * LAT : (PACK * g + r + 1) * LAT] for g in range(SETS)]
+            part = dot(jnp.concatenate(pick, axis=0).astype(BF16), taps[r, pl.ds(tap, LANES)])
+            parts = part if parts is None else parts + part
+        extra = combine(parts)
+        first = pl.multiple_of(side * (CELLS - LAT), LAT)
+        for g in range(SETS):
+            edge = total[g, pl.ds(first, LAT)] + extra[g * LAT : (g + 1) * LAT]
+            total[g, pl.ds(first, LAT)] = edge
+            for h in range(2):
+                ends[pl.ds(4 * g + 2 * h + side, LAT, stride=16), :] = edge[
+                    :, h * LANES : (h + 1) * LANES
+                ]
+
     for i in range(LAT):
         for half in range(2 * SETS):
             rows_out[i, :, half * LANES : (half + 1) * LANES] = halves[
@@ -411,58 +441,56 @@
         )
 
 
-    for side, copy in enumerate(edge_copies):
-        copy.wait_recv()
-        turn = silu(edge_in[side].astype(F32)).astype(BF16).astype(F32)
-        parts = None
-        for r in range(PACK):
-            pick = [turn[(PACK * g + r) * LAT : (PACK * g + r + 1) * LAT] for g in range(SETS)]
-            tap = 2 * side
-            part = dot(
-                jnp.concatenate(pick, axis=0).astype(BF16), taps[r, tap * LANES : (tap + 1) * LANES]
+    @pl.when(busy)
+    def _():
+        for step in EARLY:
+            row_copy(lax.rem(m + step, MEM), m).start()
+
+    build_constants(placing, diagonal, unpack)
+    channel = lax.broadcasted_iota(jnp.int32, (WIDE, WIDE), 0)
+    rim = pl.multiple_of(jnp.where(core == 0, 0, CELLS - LAT), LAT)
+
+    def choose_from(source, first_cell, more):
+        place = lax.broadcasted_iota(jnp.int32, (source.shape[1], LANES), 0) + first_cell
+
+        def choose(pair, carry):
+            rows = [pl.ds(2 * pair + n, 1) for n in range(2)]
+            hot = jnp.concatenate(
+                [jnp.where(place == cellp[at, :], 1.0, 0.0).astype(BF16) for at in rows], axis=1
             )
-            parts = part if parts is None else parts + part
-        extra = combine(parts)
-        first = 0 if side == 0 else CELLS - LAT
-        for g in range(SETS):
-            total[g, first : first + LAT] += extra[g * LAT : (g + 1) * LAT]
-            for h in range(2):
-                ends[pl.ds(4 * g + 2 * h + side, LAT, stride=16), :] = total[
-                    g, first : first + LAT, h * LANES : (h + 1) * LANES
-                ]
+            chans = jnp.concatenate([cellc[at, :] for at in rows], axis=1)
+            for g in range(SETS):
+                cells = dot(source[g * WIDE : (g + 1) * WIDE, :], hot)
+                for r in range(PACK):
+                    low, high = CHANS * r // 8 * 8, -(-CHANS * (r + 1) // 8) * 8
+                    mask = channel[low:high] - CHANS * r == chans
+                    found = jnp.sum(jnp.where(mask, cells[low:high], 0.0), axis=0, keepdims=True)
+                    for n in range(2):
+                        spot = pl.ds((PACK * g + r) * 16 + 2 * pair + n, 1)
+                        piece = found[:, n * LANES : (n + 1) * LANES]
+                        own[spot, :] = own[spot, :] + piece if more else piece
+            return carry
+
+        lax.fori_loop(0, OBS // WIDE, choose, 0, unroll=2)
+
+    mend(1 - core)
+    cell_row = lax.broadcasted_iota(jnp.int32, (BAND, WIDE), 0)
+    for g in range(SETS):
+        keep = (cell_row < rim) | (cell_row >= rim + LAT)
+        turned[g * WIDE : (g + 1) * WIDE] = jnp.where(keep, total[g], 0.0).T.astype(BF16)
+    choose_from(turned, 0, False)
+
+    mend(core)
+    for copy in stat_copies:
+        copy.start()
     ends_out[...] = ends[...].astype(BF16).reshape(LAT, 16, LANES)
     edges[m] = ends_out[m]
     for g in range(SETS):
-        turned[g * WIDE : (g + 1) * WIDE] = total[g].T.astype(BF16)
-
-    place = lax.broadcasted_iota(jnp.int32, (BAND, LANES), 0)
-    channel = lax.broadcasted_iota(jnp.int32, (WIDE, WIDE), 0)
-
-    def choose(pair, carry):
-        first = cellp[pl.ds(2 * pair, 1), :]
-        second = cellp[pl.ds(2 * pair + 1, 1), :]
-        hot = jnp.concatenate(
-            [
-                jnp.where(place == first, 1.0, 0.0).astype(BF16),
-                jnp.where(place == second, 1.0, 0.0).astype(BF16),
-            ],
-            axis=1,
-        )
-        chans = jnp.concatenate(
-            [cellc[pl.ds(2 * pair, 1), :], cellc[pl.ds(2 * pair + 1, 1), :]], axis=1
-        )
-        for g in range(SETS):
-            cells = dot(turned[g * WIDE : (g + 1) * WIDE, :], hot)
-            for r in range(PACK):
-                low, high = CHANS * r // 8 * 8, -(-CHANS * (r + 1) // 8) * 8
-                mask = channel[low:high] - CHANS * r == chans
-                found = jnp.sum(jnp.where(mask, cells[low:high], 0.0), axis=0, keepdims=True)
-                spot = (PACK * g + r) * 16 + 2 * pair
-                own[pl.ds(spot, 1), :] = found[:, :LANES]
-                own[pl.ds(spot + 1, 1), :] = found[:, LANES:]
-        return carry
-
-    lax.fori_loop(0, OBS // WIDE, choose, 0)
+        edge = jnp.concatenate(
+            [total[g, pl.ds(rim, LAT), :], jnp.zeros((LANES - LAT, WIDE), F32)], axis=0
+        )
+        turned_rim[g * WIDE : (g + 1) * WIDE] = edge.T.astype(BF16)
+    choose_from(turned_rim, rim, True)
     blocks[1, m] = own[...].astype(BF16)
 
     def arrival(slot, block):
@@ -541,15 +569,27 @@
         arrival(1, partner_mates[n]).wait_recv()
         pass_on(partner_mates[n])
 
-    for step in range(1, MEM):
-        row_copy(lax.rem(m + step, MEM), m).start()
-    for block in range(MEM):
-        arrival(mine, block).wait_recv()
-        arrival(theirs, block).wait_recv()
+    @pl.when(jnp.logical_not(busy))
+    def _():
+        for step in range(1, MEM):
+            row_copy(lax.rem(m + step, MEM), m).start()
+
     for copy in stat_copies:
         copy.wait()
     loads[-1].wait()
-    pieces = weigh(list_ref, blocks, stats, flat, table, picked, placing, stage, diagonal)
+    fill(1, blocks, stats, flat, table)
+    for block in range(MEM):
+        arrival(theirs, block).wait_recv()
+    fill(theirs, blocks, stats, flat, table)
+    for block in range(MEM):
+        arrival(mine, block).wait_recv()
+    fill(mine, blocks, stats, flat, table)
+    @pl.when(busy)
+    def _():
+        for step in LATE:
+            row_copy(lax.rem(m + step, MEM), m).start()
+
+    pieces = weigh(list_ref, table, picked, placing, stage, diagonal)
 
     for step in range(1, MEM):
         other = lax.rem(m + step, MEM)
@@ -598,6 +638,7 @@
             pltpu.VMEM((SETS, BAND, WIDE), F32),
             pltpu.VMEM((2 * SETS, BAND, LANES), F32),
             pltpu.VMEM((SETS * WIDE, BAND), BF16),
+            pltpu.VMEM((SETS * WIDE, LANES), BF16),
             pltpu.VMEM((16, LANES), jnp.int32),
             pltpu.VMEM((16, LANES), jnp.int32),
             pltpu.VMEM((OWN * 16, LANES), F32),
@@ -606,7 +647,7 @@
             pltpu.VMEM((LAT, SLOT, SETS * WIDE), BF16),
             pltpu.VMEM((LAT * 16, LANES), F32),
             pltpu.VMEM((LAT, 16, LANES), BF16),
-            pltpu.VMEM((3 * MEM * OWN * 16, LANES), F32),
+            pltpu.VMEM((MEM * OWN * 16, LANES), F32),
             pltpu.VMEM((3 * OBS, LANES), F32),
             pltpu.VMEM((GROUP, GROUPS * OBS_COL, LANES), F32),
             pltpu.VMEM((GROUP * LANES, 4 * WIDE), BF16),

time: 65.9 us -> 61 us (0.926)
  Pallas kernels: 63.4 us -> 58.5 us
    pallas_call x1, Pallas kernels: 63.4 us -> 58.5 us  [exchange(): pl.pallas_call(exchange_kernel, out_shape=jax.ShapeDtypeStruct((MEMBERS *...]
where the time goes in v3:
time: 61 us; the launch traced here: 60.8 us
  Pallas kernels  58.5 us (96%)
  local copies, waits for them, and re-layouts  2.33 us (4%)
    pallas_call x1, Pallas kernels, exchange(): pl.pallas_call(exchange_kernel, out_shape=jax.ShapeDtypeStruct((MEMBERS *...  58.5 us
    unnamed x1, local copies, waits for them, and re-layouts  2.33 us

profile of v3, /device:TPU:1, one launch (start us, length us, event | category | flops | bytes accessed | tf_op | source)
XLA Modules:
  0.0 60.8 jit_solution(14975891308545504384)
XLA Ops:
  0.0 58.5 %shard_map.73 = f32[2160,78]{1,0:T(8,128)} custom-call(bf16[6,45,8,78]{3,2,1,0:T(8,128)(2,1)} %bitcast.8, bf16[3,3,78,78]{3,2,1,0:T(8,128)(2,1)} %w_hbm.1, f32[1,78]{1,0:T(1,128)} %bitcast.13, s32[16,128]{1,0:T(8,128)} %bitcast.10, f32[16,128]{1,0:T(8,128)} %bitcast.11, f32[16,128]{1,0:T(8,128)} %bitcast.12, s32[45,1,64]{2,1,0:T(1,128)} %bitcast.9), custom_call_target="tpu_custom_call" | custom-call | tf_op jit(solution)/shard_map/pallas_call | solution.py:619
  58.5 2.3 %copy.11 = f32[48,1,45,78]{3,1,2,0:T(1,128)} copy(f32[48,1,45,78]{3,1,2,0:T(1,128)} %bitcast.7) | data formatting | bytes 1347840

commit v4 on v3

--- a/solution.py
+++ b/solution.py
@@ -25,8 +25,8 @@
 BAND = 384
 WIDE = 2 * LANES
 SLOT = 48
-EARLY = (3, 4, 5)
-LATE = (1, 2, 6, 7)
+EARLY = (1, 2, 3, 5, 6, 7)
+LATE = (4,)
 F32 = jnp.float32
 BF16 = jnp.bfloat16
 MESH = pl.DeviceIdType.MESH
@@ -79,15 +79,16 @@
     member = row < MEMBERS
     for s in range(GROUP):
         inside = (col >= s * MEMBERS) & (col < (s + 1) * MEMBERS)
+        same = col - s * MEMBERS == row
         kinds = (
-            member & (col - s * MEMBERS == row),
-            member & inside,
-            ((row == MEMBERS) | (row == MEMBERS + 2)) & inside,
-            ((row == MEMBERS + 1) | (row == MEMBERS + 3)) & inside,
+            jnp.where(same, MEMBERS - 1.0, -1.0),
+            jnp.where(member, -1.0, jnp.where((row == MEMBERS) | (row == MEMBERS + 2), MEMBERS, 0.0)),
+            jnp.where((row == MEMBERS + 1) | (row == MEMBERS + 3), 1.0, 0.0),
         )
         for n, kind in enumerate(kinds):
+            keep = inside & member if n == 0 else inside
             placing[s * LANES : (s + 1) * LANES, n * WIDE : (n + 1) * WIDE] = jnp.where(
-                kind, 1.0, 0.0
+                keep, kind, 0.0
             ).astype(BF16)
 
 
@@ -108,7 +109,7 @@
     lax.fori_loop(0, 16, turn, 0, unroll=8)
 
 
-def weigh(list_ref, table, picked, placing, stage, diagonal):
+def weigh(list_ref, table, picked, placing, stage, diagonal, between):
     def gather(q, carry):
         base = q * OBS_COL
         for s in range(GROUP):
@@ -118,6 +119,7 @@
         return carry
 
     lax.fori_loop(0, GROUPS, gather, 0)
+    between()
     found = jnp.concatenate([picked[s].astype(BF16) for s in range(GROUP)], axis=1)
     stage[...] = dot(found, placing[...])
 
@@ -136,10 +138,9 @@
     grams, proj, traces = [], [], []
     for q in every:
         rows = slice(q * OBS_COL, (q + 1) * OBS_COL)
-        mean = stage[rows, WIDE : 2 * WIDE] * (1.0 / MEMBERS)
-        pert = stage[rows, :WIDE] - mean
-        depart = stage[rows, 2 * WIDE : 3 * WIDE] - mean
-        scaled = pert * stage[rows, 3 * WIDE :]
+        pert = stage[rows, :WIDE] * (1.0 / MEMBERS)
+        depart = stage[rows, WIDE : 2 * WIDE] * (1.0 / MEMBERS)
+        scaled = pert * stage[rows, 2 * WIDE :]
         proj.append(jnp.sum(scaled * depart, axis=0, keepdims=True))
         traces.append(jnp.sum(scaled * pert, axis=0, keepdims=True))
         high, low = split(pert)
@@ -217,7 +218,7 @@
     return pieces
 
 
-def apply(pieces, states, edges, unpack, columns, done, out):
+def apply(pieces, states, edges, unpack, columns, out):
     for source in range(MEM):
         for g in range(SETS):
             parts = dot(states[source, :, g * WIDE : (g + 1) * WIDE], unpack[...])
@@ -240,12 +241,12 @@
 
     for q in range(GROUPS):
         field = columns[q * GROUP * MEMBERS : q * GROUP * MEMBERS + WIDE, :].astype(BF16)
-        result = dot(pieces[q][0], field) + dot(pieces[q][1], field)
+        both = dot(jnp.concatenate(pieces[q], axis=0), field)
+        result = both[:WIDE] + both[WIDE:]
         for s in range(GROUP):
-            done[pl.ds(q * GROUP + s, MEMBERS, stride=WIDTH), :] = result[
+            out[pl.ds(q * GROUP + s, MEMBERS, stride=WIDTH), :] = result[
                 s * MEMBERS : (s + 1) * MEMBERS
             ]
-    out[...] = done[:, :CHANS]
 
 
 def exchange_kernel(
@@ -254,7 +255,7 @@
     lat_ref, w_ref, bias_ref, cell_ref, list_ref, blocks, stats, states, edges,
     field, act, wpad, taps, total, halves, turned, turned_rim, cellp, cellc,
     own, edge_out, edge_in, rows_out, ends, ends_out,
-    flat, table, picked, placing, stage, columns, diagonal, unpack, done,
+    flat, table, picked, placing, stage, columns, diagonal, unpack,
     loaded, edge_sent, edge_got, stat_sent, stat_got, mate_sent, sib_sent, outer_sent, block_got,
     state_sent, state_got, end_sent, end_got,
 ):
@@ -541,7 +542,7 @@
 
     @pl.when(far)
     def _():
-        for step in range(MEM):
+        for step in range(1, MEM, 2):
             to = lax.rem(m + step, MEM)
             outward(m, to, to).start()
 
@@ -574,6 +575,25 @@
         for step in range(1, MEM):
             row_copy(lax.rem(m + step, MEM), m).start()
 
+    beside = m + 1 - 2 * lax.rem(m, 2)
+
+    def hand(block, sent):
+        return pltpu.make_async_remote_copy(
+            src_ref=blocks.at[mine, block],
+            dst_ref=blocks.at[mine, block],
+            send_sem=outer_sent.at[sent],
+            recv_sem=block_got.at[mine, block],
+            device_id={"mem": beside},
+            device_id_type=MESH,
+        )
+
+    @pl.when(far)
+    def _():
+        for step in range(1, MEM, 2):
+            block = lax.rem(m + step, MEM)
+            arrival(mine, block).wait_recv()
+            hand(block, lax.rem(m + step - 1, MEM)).start()
+
     for copy in stat_copies:
         copy.wait()
     loads[-1].wait()
@@ -581,21 +601,30 @@
     for block in range(MEM):
         arrival(theirs, block).wait_recv()
     fill(theirs, blocks, stats, flat, table)
-    for block in range(MEM):
-        arrival(mine, block).wait_recv()
+    @pl.when(far)
+    def _():
+        for step in range(0, MEM, 2):
+            arrival(mine, lax.rem(m + step, MEM)).wait_recv()
+
+    @pl.when(jnp.logical_not(far))
+    def _():
+        for block in range(MEM):
+            arrival(mine, block).wait_recv()
+
     fill(mine, blocks, stats, flat, table)
-    @pl.when(busy)
-    def _():
-        for step in LATE:
-            row_copy(lax.rem(m + step, MEM), m).start()
-
-    pieces = weigh(list_ref, table, picked, placing, stage, diagonal)
+    def send_late():
+        @pl.when(busy)
+        def _():
+            for step in LATE:
+                row_copy(lax.rem(m + step, MEM), m).start()
+
+    pieces = weigh(list_ref, table, picked, placing, stage, diagonal, send_late)
 
     for step in range(1, MEM):
         other = lax.rem(m + step, MEM)
         row_copy(other, other).wait_recv()
         end_copy(other, other).wait_recv()
-    apply(pieces, states, edges, unpack, columns, done, out)
+    apply(pieces, states, edges, unpack, columns, out)
 
     for copy in edge_copies:
         copy.wait_send()
@@ -618,7 +647,7 @@
     dma = pltpu.SemaphoreType.DMA
     return pl.pallas_call(
         exchange_kernel,
-        out_shape=jax.ShapeDtypeStruct((MEMBERS * WIDTH, CHANS), F32),
+        out_shape=jax.ShapeDtypeStruct((MEMBERS * WIDTH, LANES), F32),
         in_specs=[hbm] * 7,
         out_specs=vmem,
         scratch_shapes=[
@@ -650,12 +679,11 @@
             pltpu.VMEM((MEM * OWN * 16, LANES), F32),
             pltpu.VMEM((3 * OBS, LANES), F32),
             pltpu.VMEM((GROUP, GROUPS * OBS_COL, LANES), F32),
-            pltpu.VMEM((GROUP * LANES, 4 * WIDE), BF16),
-            pltpu.VMEM((GROUPS * OBS_COL, 4 * WIDE), F32),
+            pltpu.VMEM((GROUP * LANES, 3 * WIDE), BF16),
+            pltpu.VMEM((GROUPS * OBS_COL, 3 * WIDE), F32),
             pltpu.VMEM((SLOT * MEMBERS, LANES), F32),
             pltpu.VMEM((WIDE, WIDE), BF16),
             pltpu.VMEM((WIDE, PACK * LANES), BF16),
-            pltpu.VMEM((MEMBERS * WIDTH, LANES), F32),
             dma((7,)),
             dma((2,)),
             dma((2,)),
@@ -686,7 +714,7 @@
         obs_weight.reshape(16, LANES),
         obs_list.reshape(WIDTH, 1, OBS_COL),
     )
-    return jnp.transpose(result.reshape(MEMBERS, WIDTH, 1, CHANS), (0, 2, 1, 3))
+    return jnp.transpose(result[:, :CHANS].reshape(MEMBERS, WIDTH, 1, CHANS), (0, 2, 1, 3))
 
 
 def solution(mesh):

time: 61 us -> 58.3 us (0.956)
  Pallas kernels: 58.5 us -> 55.8 us
    pallas_call x1, Pallas kernels: 58.5 us -> 55.8 us  [exchange(): pl.pallas_call(exchange_kernel, out_shape=jax.ShapeDtypeStruct((MEMBERS *...]
where the time goes in v4:
time: 58.3 us; the launch traced here: 58.1 us
  Pallas kernels  55.8 us (96%)
  local copies, waits for them, and re-layouts  2.33 us (4%)
    pallas_call x1, Pallas kernels, exchange(): pl.pallas_call(exchange_kernel, out_shape=jax.ShapeDtypeStruct((MEMBERS *...  55.8 us
    unnamed x1, local copies, waits for them, and re-layouts  2.33 us

profile of v4, /device:TPU:1, one launch (start us, length us, event | category | flops | bytes accessed | tf_op | source)
XLA Modules:
  0.0 58.1 jit_solution(2781798783440323234)
XLA Ops:
  0.0 55.8 %shard_map.73 = f32[2160,128]{1,0:T(8,128)} custom-call(bf16[6,45,8,78]{3,2,1,0:T(8,128)(2,1)} %bitcast.9, bf16[3,3,78,78]{3,2,1,0:T(8,128)(2,1)} %w_hbm.1, f32[1,78]{1,0:T(1,128)} %bitcast.14, s32[16,128]{1,0:T(8,128)} %bitcast.11, f32[16,128]{1,0:T(8,128)} %bitcast.12, f32[16,128]{1,0:T(8,128)} %bitcast.13, s32[45,1,64]{2,1,0:T(1,128)} %bitcast.10), custom_call_target="tpu_custom_call" | custom-call | tf_op jit(solution)/shard_map/pallas_call | solution.py:648
  55.8 2.3 %copy.11 = f32[48,1,45,78]{3,1,2,0:T(1,128)} copy(f32[48,1,45,78]{3,1,2,0:T(1,128)} %bitcast.8) | data formatting | bytes 1347840

commit v5 on v4

--- a/solution.py
+++ b/solution.py
@@ -481,9 +481,9 @@
         turned[g * WIDE : (g + 1) * WIDE] = jnp.where(keep, total[g], 0.0).T.astype(BF16)
     choose_from(turned, 0, False)
 
-    mend(core)
     for copy in stat_copies:
         copy.start()
+    mend(core)
     ends_out[...] = ends[...].astype(BF16).reshape(LAT, 16, LANES)
     edges[m] = ends_out[m]
     for g in range(SETS):
@@ -540,6 +540,8 @@
     mates = [half + lax.rem(m + step, 4) for step in range(1, 4)]
     partner_mates = [partner_half + lax.rem(m + step, 4) for step in range(1, 4)]
 
+    along(m, 3, partner).start()
+
     @pl.when(far)
     def _():
         for step in range(1, MEM, 2):
@@ -553,7 +555,6 @@
         def _():
             outward(block, block, m).start()
 
-    along(m, 3, partner).start()
     for n in range(3):
         along(m, n, mates[n]).start()
     pass_on(m)
@@ -587,6 +588,8 @@
             device_id_type=MESH,
         )
 
+    fill(1, blocks, stats, flat, table)
+
     @pl.when(far)
     def _():
         for step in range(1, MEM, 2):
@@ -597,7 +600,6 @@
     for copy in stat_copies:
         copy.wait()
     loads[-1].wait()
-    fill(1, blocks, stats, flat, table)
     for block in range(MEM):
         arrival(theirs, block).wait_recv()
     fill(theirs, blocks, stats, flat, table)

time: 58.3 us -> 58.1 us (level)
  Pallas kernels: 55.8 us -> 55.1 us
    pallas_call x1, Pallas kernels: 55.8 us -> 55.1 us  [exchange(): pl.pallas_call(exchange_kernel, out_shape=jax.ShapeDtypeStruct((MEMBERS *...]
where the time goes in v5:
time: 58.1 us; the launch traced here: 57.4 us
  Pallas kernels  55.1 us (95%)
  local copies, waits for them, and re-layouts  2.33 us (4%)
    pallas_call x1, Pallas kernels, exchange(): pl.pallas_call(exchange_kernel, out_shape=jax.ShapeDtypeStruct((MEMBERS *...  55.1 us
    unnamed x1, local copies, waits for them, and re-layouts  2.33 us

profile of v5, /device:TPU:1, one launch (start us, length us, event | category | flops | bytes accessed | tf_op | source)
XLA Modules:
  0.0 57.4 jit_solution(1457811272556643307)
XLA Ops:
  0.0 55.1 %shard_map.73 = f32[2160,128]{1,0:T(8,128)} custom-call(bf16[6,45,8,78]{3,2,1,0:T(8,128)(2,1)} %bitcast.9, bf16[3,3,78,78]{3,2,1,0:T(8,128)(2,1)} %w_hbm.1, f32[1,78]{1,0:T(1,128)} %bitcast.14, s32[16,128]{1,0:T(8,128)} %bitcast.11, f32[16,128]{1,0:T(8,128)} %bitcast.12, f32[16,128]{1,0:T(8,128)} %bitcast.13, s32[45,1,64]{2,1,0:T(1,128)} %bitcast.10), custom_call_target="tpu_custom_call" | custom-call | tf_op jit(solution)/shard_map/pallas_call | solution.py:650
  55.1 2.3 %copy.11 = f32[48,1,45,78]{3,1,2,0:T(1,128)} copy(f32[48,1,45,78]{3,1,2,0:T(1,128)} %bitcast.8) | data formatting | bytes 1347840
